TPU v7x, 32 devices: a whole 2x2x4 slice. The times are simulated.
32 devices in a mesh: seq: 32 (over z, y, x, core).
Axes of the slice: x: 2, y: 2, z: 4, core: 2. Of those that a mesh axis runs over, the one named last changes fastest.
Arguments:
- activations: bfloat16 [65536, 384], P('seq'), may hold values from -6 to 6
- conv_weight: bfloat16 [4, 3, 384, 384], replicated, may hold values from -0.1875 to 0.1875
- conv_bias: float32 [4, 384], replicated, may hold values from -3 to 3
- conv_gain: float32 [4, 384], replicated, may hold values from 0.1 to 1.9
- mlp_gain: float32 [4, 384], replicated, may hold values from 0.1 to 1.9
- w_in: bfloat16 [4, 384, 768], replicated, may hold values from -0.3125 to 0.3125
- w_out: bfloat16 [4, 768, 384], replicated, may hold values from -0.21875 to 0.21875
Outputs:
- channel_major: bfloat16 [384, 65536], P('seq')
All inputs are finite; a program needn't handle non-finite values.
Results may differ from a plain program's by a relative error of at most 0.015.
Values may be sent and summed in bfloat16 or wider, within the bound.
No kernel may reach another device: no remote copies, remote signals or barrier semaphores. Data moves between devices by JAX's collectives and lax.ppermute only.
A program may use at most 64 MiB of HBM per device.

v0:
```python
import jax
import jax.numpy as jnp
from jax import lax
from jax.sharding import PartitionSpec as P


def from_behind(block, axis, distance):
    devices = range(lax.axis_size(axis))
    route = [(i - distance, i) for i in devices if i - distance in devices]
    return lax.ppermute(block, axis, route)


def rms_scale(values, gain):
    wide = values.astype(jnp.float32)
    inverse = lax.rsqrt(jnp.mean(wide * wide, axis=-1, keepdims=True) + 1e-06)
    return (wide * inverse * gain[None, :]).astype(jnp.bfloat16)


def one_layer(state, taps, bias, gain_conv, gain_mlp, proj_in, proj_out, distance):
    normed = rms_scale(state, gain_conv)
    earlier = from_behind(normed, "seq", distance)
    later = from_behind(normed, "seq", -distance)
    pre = jnp.dot(normed, taps[1], preferred_element_type=jnp.float32)
    pre = pre + jnp.dot(earlier, taps[0], preferred_element_type=jnp.float32)
    pre = pre + jnp.dot(later, taps[2], preferred_element_type=jnp.float32)
    pre = pre + bias[None, :]
    middle = (state.astype(jnp.float32) + jax.nn.gelu(pre, approximate=False)).astype(jnp.bfloat16)
    inner = rms_scale(middle, gain_mlp)
    hidden = jax.nn.gelu(
        jnp.dot(inner, proj_in, preferred_element_type=jnp.float32), approximate=False
    ).astype(jnp.bfloat16)
    return (
        middle.astype(jnp.float32) + jnp.dot(hidden, proj_out, preferred_element_type=jnp.float32)
    ).astype(jnp.bfloat16)


def shards(activations, conv_weight, conv_bias, conv_gain, mlp_gain, w_in, w_out):
    state = activations
    for layer in range(conv_weight.shape[0]):
        state = one_layer(
            state,
            conv_weight[layer],
            conv_bias[layer],
            conv_gain[layer],
            mlp_gain[layer],
            w_in[layer],
            w_out[layer],
            2**layer,
        )
    return lax.all_to_all(state.T, "seq", split_axis=0, concat_axis=1, tiled=True)


def solution(mesh):
    in_specs = (P("seq", None), P(), P(), P(), P(), P(), P())
    out_specs = P("seq", None)
    return jax.shard_map(shards, mesh=mesh, in_specs=in_specs, out_specs=out_specs, check_vma=False)
```

profile of v0, /device:TPU:0, one launch (start us, length us, event | category | flops | bytes accessed | tf_op | source)
XLA Modules:
  0.0 412.8 jit_solution(7692534820497674014)
XLA Ops:
  1.5 1.7 copy.11
  4.0 2.5 collective-permute-start
  9.0 2.0 fusion.201
  11.0 2.0 fusion.199
  13.7 10.5 %fusion.46 = (f32[2048]{0:T(1024)S(1)}, bf16[2048,384]{0,1:T(8,128)(2,1)}) fusion(f32[384]{0:T(512)S(1)} %get-tuple-element.11, bf16[2048,384]{0,1:T(8,128)(2,1)S(1)} %collective-permute-done.1, bf16[4,3,384,384]{3,2,1,0:T(8,128)(2,1)} %param.8, f32[2048,384]{0,1:T(8,128)S(1)} %fusion.201, f32[2048,384]{0,1:T(8,128)S(1)} %fusion.199, ...), kind=kOutput, calls=%fused_computation.110 | convolution fusion | flops 661387264 | bytes 11314688 | tf_op jit(solution)/shard_map/dot_general | solution.py:25
  24.3 20.1 %fusion.50 = (f32[2048]{0:T(1024)S(1)}, bf16[2048,384]{0,1:T(8,128)(2,1)}) fusion(bf16[4,768,384]{2,1,0:T(8,128)(2,1)} %param.13, bf16[2048,384]{0,1:T(8,128)(2,1)} %get-tuple-element.18, f32[384]{0:T(512)} %get-tuple-element.7, f32[2048]{0:T(1024)S(1)} %add_rsqrt_fusion.6, bf16[4,384,768]{2,1,0:T(8,128)(2,1)} %param.12), kind=kOutput, calls=%fused_computation.114 | convolution fusion | flops 2526017536 | bytes 5916672 | tf_op jit(solution)/shard_map/dot_general | solution.py:33
  44.4 1.8 fusion.52
  46.2 35.8 %collective-permute-start.2 = (bf16[2048,384]{0,1:T(8,128)(2,1)S(1)}, bf16[2048,384]{0,1:T(8,128)(2,1)S(1)}, u32[]{:S(2)}, u32[]{:S(2)}) collective-permute-start(bf16[2048,384]{0,1:T(8,128)(2,1)S(1)} %fusion.52), channel_id=1, source_target_pairs={{0,2},{1,3},{2,4},{3,5},{4,6},{5,7},{6,8},{7,9},{8,10},{9,11},{10,... | collective-permute-start | bytes 4718600 | tf_op jit(solution)/shard_map/ppermute | solution.py:10
  84.3 63.8 %collective-permute-done.2 = bf16[2048,384]{0,1:T(8,128)(2,1)S(1)} collective-permute-done((bf16[2048,384]{0,1:T(8,128)(2,1)S(1)}, bf16[2048,384]{0,1:T(8,128)(2,1)S(1)}, u32[]{:S(2)}, u32[]{:S(2)}) %collective-permute-start.2) | collective-permute-done | bytes 1572896 | tf_op jit(solution)/shard_map/ppermute | solution.py:10
  149.2 9.5 %fusion.56 = (f32[2048]{0:T(1024)S(1)}, bf16[2048,384]{0,1:T(8,128)(2,1)}) fusion(f32[384]{0:T(512)S(1)} %copy-done.9, bf16[2048,384]{0,1:T(8,128)(2,1)S(1)} %collective-permute-done.3, bf16[4,3,384,384]{3,2,1,0:T(8,128)(2,1)S(1)} %copy-done, f32[2048,384]{0,1:T(8,128)S(1)} %fusion.196, f32[2048,384]{0,1:T(8,128)S(1)} %fusion.194, ...), kind=kOutput, calls=%fused_computation.120 | convolution fusion | flops 661387264 | bytes 11315200 | tf_op jit(solution)/shard_map/dot_general | solution.py:25
  158.7 19.7 %fusion.60 = (f32[2048]{0:T(1024)S(1)}, bf16[2048,384]{0,1:T(8,128)(2,1)}) fusion(bf16[4,768,384]{2,1,0:T(8,128)(2,1)} %param.13, bf16[2048,384]{0,1:T(8,128)(2,1)} %get-tuple-element.22, f32[384]{0:T(512)} %get-tuple-element.6, f32[2048]{0:T(1024)S(1)} %add_rsqrt_fusion.4, bf16[4,384,768]{2,1,0:T(8,128)(2,1)} %param.12), kind=kOutput, calls=%fused_computation.124 | convolution fusion | flops 2526017536 | bytes 5916672 | tf_op jit(solution)/shard_map/dot_general | solution.py:33
  178.4 1.8 fusion.62
  183.9 63.2 %collective-permute-done.4 = bf16[2048,384]{0,1:T(8,128)(2,1)S(1)} collective-permute-done((bf16[2048,384]{0,1:T(8,128)(2,1)S(1)}, bf16[2048,384]{0,1:T(8,128)(2,1)S(1)}, u32[]{:S(2)}, u32[]{:S(2)}) %collective-permute-start.4) | collective-permute-done | bytes 1572896 | tf_op jit(solution)/shard_map/ppermute | solution.py:10
  248.2 9.5 %fusion.66 = (f32[2048]{0:T(1024)S(1)}, bf16[2048,384]{0,1:T(8,128)(2,1)}) fusion(f32[384]{0:T(512)S(1)} %copy-done.8, bf16[2048,384]{0,1:T(8,128)(2,1)S(1)} %collective-permute-done.5, bf16[4,3,384,384]{3,2,1,0:T(8,128)(2,1)S(1)} %copy-done, f32[2048,384]{0,1:T(8,128)S(1)} %fusion.191, f32[2048,384]{0,1:T(8,128)S(1)} %fusion.189, ...), kind=kOutput, calls=%fused_computation.130 | convolution fusion | flops 661387264 | bytes 11315200 | tf_op jit(solution)/shard_map/dot_general | solution.py:25
  257.6 19.8 %fusion.70 = (f32[2048]{0:T(1024)S(1)}, bf16[2048,384]{0,1:T(8,128)(2,1)}) fusion(bf16[4,768,384]{2,1,0:T(8,128)(2,1)} %param.13, bf16[2048,384]{0,1:T(8,128)(2,1)} %get-tuple-element.26, f32[384]{0:T(512)} %get-tuple-element.8, f32[2048]{0:T(1024)S(1)} %add_rsqrt_fusion.2, bf16[4,384,768]{2,1,0:T(8,128)(2,1)} %param.12), kind=kOutput, calls=%fused_computation.134 | convolution fusion | flops 2526017536 | bytes 5916672 | tf_op jit(solution)/shard_map/dot_general | solution.py:33
  277.4 1.8 fusion.72
  279.2 8.4 %collective-permute-start.6 = (bf16[2048,384]{0,1:T(8,128)(2,1)S(1)}, bf16[2048,384]{0,1:T(8,128)(2,1)S(1)}, u32[]{:S(2)}, u32[]{:S(2)}) collective-permute-start(bf16[2048,384]{0,1:T(8,128)(2,1)S(1)} %fusion.72), channel_id=1, source_target_pairs={{0,8},{1,9},{2,10},{3,11},{4,12},{5,13},{6,14},{7,15},{8,16},{9,17... | collective-permute-start | bytes 4718600 | tf_op jit(solution)/shard_map/ppermute | solution.py:10
  290.0 31.4 %collective-permute-done.6 = bf16[2048,384]{0,1:T(8,128)(2,1)S(1)} collective-permute-done((bf16[2048,384]{0,1:T(8,128)(2,1)S(1)}, bf16[2048,384]{0,1:T(8,128)(2,1)S(1)}, u32[]{:S(2)}, u32[]{:S(2)}) %collective-permute-start.6) | collective-permute-done | bytes 1572896 | tf_op jit(solution)/shard_map/ppermute | solution.py:10
  322.4 3.2 collective-permute-done.7
  325.6 9.5 %fusion.76 = (f32[2048]{0:T(1024)S(1)}, bf16[2048,384]{0,1:T(8,128)(2,1)}) fusion(f32[384]{0:T(512)S(1)} %copy-done.7, bf16[2048,384]{0,1:T(8,128)(2,1)S(1)} %collective-permute-done.7, bf16[4,3,384,384]{3,2,1,0:T(8,128)(2,1)S(1)} %copy-done, f32[2048,384]{0,1:T(8,128)S(1)} %fusion.186, f32[2048,384]{0,1:T(8,128)S(1)} %fusion.184, ...), kind=kOutput, calls=%fused_computation.140 | convolution fusion | flops 661387264 | bytes 11315200 | tf_op jit(solution)/shard_map/dot_general | solution.py:25
  335.1 19.5 %fusion.124 = bf16[384,2048]{1,0:T(8,128)(2,1)} fusion(bf16[2048,384]{0,1:T(8,128)(2,1)} %get-tuple-element.30, f32[384]{0:T(512)S(1)} %copy-done.6, f32[2048]{0:T(1024)S(1)} %add_rsqrt_fusion, bf16[4,768,384]{2,1,0:T(8,128)(2,1)} %param.13, bf16[4,384,768]{2,1,0:T(8,128)(2,1)} %param.12), kind=kOutput, calls=%fused_computation.212 | convolution fusion | flops 2523660288 | bytes 5907968 | tf_op jit(solution)/shard_map/dot_general | solution.py:33
  354.6 2.4 all_to_all.14
  357.0 51.9 %all_to_all.19 = bf16[32,12,2048]{2,1,0:T(8,128)(2,1)S(1)} all-to-all(bf16[32,12,2048]{2,1,0:T(8,128)(2,1)S(1)} %all_to_all.14), channel_id=1, replica_groups=mesh['seq'=32] {'seq'}, dimensions={0} | all-to-all | bytes 3145728 | tf_op jit(solution)/shard_map/all_to_all | solution.py:50
  410.0 2.5 copy.13
  (50 shorter events, 18.2 us)
Async XLA Ops:
  3.2 4.5 %copy-start.4 = (f32[4,384]{1,0:T(4,128)S(1)}, f32[4,384]{1,0:T(4,128)}, u32[]{:S(2)}) copy-start(f32[4,384]{1,0:T(4,128)} %param.9) | copy-start | bytes 18436
  3.2 5.2 %copy-start.5 = (f32[4,384]{1,0:T(4,128)S(1)}, f32[4,384]{1,0:T(4,128)}, u32[]{:S(2)}) copy-start(f32[4,384]{1,0:T(4,128)} %param.11) | copy-start | bytes 18436
  4.0 7.0 %collective-permute-start = (bf16[2048,384]{0,1:T(8,128)(2,1)S(1)}, bf16[2048,384]{0,1:T(8,128)(2,1)S(1)}, u32[]{:S(2)}, u32[]{:S(2)}) collective-permute-start(bf16[2048,384]{0,1:T(8,128)(2,1)S(1)} %fusion.42), channel_id=1, source_target_pairs={{0,1},{1,2},{2,3},{3,4},{4,5},{5,6},{6,7},{7,8},{8,9},{9,10},{10,1... | collective-permute-start | bytes 4718600 | tf_op jit(solution)/shard_map/ppermute | solution.py:10
  6.4 7.3 %collective-permute-start.1 = (bf16[2048,384]{0,1:T(8,128)(2,1)S(1)}, bf16[2048,384]{0,1:T(8,128)(2,1)S(1)}, u32[]{:S(2)}, u32[]{:S(2)}) collective-permute-start(bf16[2048,384]{0,1:T(8,128)(2,1)S(1)} %fusion.42), channel_id=1, source_target_pairs={{1,0},{2,1},{3,2},{4,3},{5,4},{6,5},{7,6},{8,7},{9,8},{10,9},{11,1... | collective-permute-start | bytes 4718600 | tf_op jit(solution)/shard_map/ppermute | solution.py:10
  24.3 59.0 %copy-start = (bf16[4,3,384,384]{3,2,1,0:T(8,128)(2,1)S(1)}, bf16[4,3,384,384]{3,2,1,0:T(8,128)(2,1)}, u32[]{:S(2)}) copy-start(bf16[4,3,384,384]{3,2,1,0:T(8,128)(2,1)} %param.8) | copy-start | bytes 10616836
  46.2 101.9 %collective-permute-start.2 = (bf16[2048,384]{0,1:T(8,128)(2,1)S(1)}, bf16[2048,384]{0,1:T(8,128)(2,1)S(1)}, u32[]{:S(2)}, u32[]{:S(2)}) collective-permute-start(bf16[2048,384]{0,1:T(8,128)(2,1)S(1)} %fusion.52), channel_id=1, source_target_pairs={{0,2},{1,3},{2,4},{3,5},{4,6},{5,7},{6,8},{7,9},{8,10},{9,11},{10,... | collective-permute-start | bytes 4718600 | tf_op jit(solution)/shard_map/ppermute | solution.py:10
  82.0 67.2 %collective-permute-start.3 = (bf16[2048,384]{0,1:T(8,128)(2,1)S(1)}, bf16[2048,384]{0,1:T(8,128)(2,1)S(1)}, u32[]{:S(2)}, u32[]{:S(2)}) collective-permute-start(bf16[2048,384]{0,1:T(8,128)(2,1)S(1)} %fusion.52), channel_id=1, source_target_pairs={{2,0},{3,1},{4,2},{5,3},{6,4},{7,5},{8,6},{9,7},{10,8},{11,9},{12,... | collective-permute-start | bytes 4718600 | tf_op jit(solution)/shard_map/ppermute | solution.py:10
  84.3 64.9 %copy-start.2 = (bf16[2048,384]{0,1:T(8,128)(2,1)S(1)}, bf16[2048,384]{0,1:T(8,128)(2,1)}, u32[]{:S(2)}) copy-start(bf16[2048,384]{0,1:T(8,128)(2,1)} %get-tuple-element.20) | copy-start | bytes 4718596
  84.3 64.9 %copy-start.9 = (f32[384]{0:T(512)S(1)}, f32[384]{0:T(512)}, u32[]{:S(2)}) copy-start(f32[384]{0:T(512)} %get-tuple-element.10) | copy-start | bytes 4612
  180.2 66.9 %collective-permute-start.4 = (bf16[2048,384]{0,1:T(8,128)(2,1)S(1)}, bf16[2048,384]{0,1:T(8,128)(2,1)S(1)}, u32[]{:S(2)}, u32[]{:S(2)}) collective-permute-start(bf16[2048,384]{0,1:T(8,128)(2,1)S(1)} %fusion.62), channel_id=1, source_target_pairs={{0,4},{1,5},{2,6},{3,7},{4,8},{5,9},{6,10},{7,11},{8,12},{9,13},{1... | collective-permute-start | bytes 4718600 | tf_op jit(solution)/shard_map/ppermute | solution.py:10
  181.6 66.6 %collective-permute-start.5 = (bf16[2048,384]{0,1:T(8,128)(2,1)S(1)}, bf16[2048,384]{0,1:T(8,128)(2,1)S(1)}, u32[]{:S(2)}, u32[]{:S(2)}) collective-permute-start(bf16[2048,384]{0,1:T(8,128)(2,1)S(1)} %fusion.62), channel_id=1, source_target_pairs={{4,0},{5,1},{6,2},{7,3},{8,4},{9,5},{10,6},{11,7},{12,8},{13,9},{1... | collective-permute-start | bytes 4718600 | tf_op jit(solution)/shard_map/ppermute | solution.py:10
  183.9 64.2 %copy-start.3 = (bf16[2048,384]{0,1:T(8,128)(2,1)S(1)}, bf16[2048,384]{0,1:T(8,128)(2,1)}, u32[]{:S(2)}) copy-start(bf16[2048,384]{0,1:T(8,128)(2,1)} %get-tuple-element.24) | copy-start | bytes 4718596
  183.9 64.2 %copy-start.8 = (f32[384]{0:T(512)S(1)}, f32[384]{0:T(512)}, u32[]{:S(2)}) copy-start(f32[384]{0:T(512)} %get-tuple-element.12) | copy-start | bytes 4612
  279.2 42.2 %collective-permute-start.6 = (bf16[2048,384]{0,1:T(8,128)(2,1)S(1)}, bf16[2048,384]{0,1:T(8,128)(2,1)S(1)}, u32[]{:S(2)}, u32[]{:S(2)}) collective-permute-start(bf16[2048,384]{0,1:T(8,128)(2,1)S(1)} %fusion.72), channel_id=1, source_target_pairs={{0,8},{1,9},{2,10},{3,11},{4,12},{5,13},{6,14},{7,15},{8,16},{9,17... | collective-permute-start | bytes 4718600 | tf_op jit(solution)/shard_map/ppermute | solution.py:10
  287.7 37.9 %collective-permute-start.7 = (bf16[2048,384]{0,1:T(8,128)(2,1)S(1)}, bf16[2048,384]{0,1:T(8,128)(2,1)S(1)}, u32[]{:S(2)}, u32[]{:S(2)}) collective-permute-start(bf16[2048,384]{0,1:T(8,128)(2,1)S(1)} %fusion.72), channel_id=1, source_target_pairs={{8,0},{9,1},{10,2},{11,3},{12,4},{13,5},{14,6},{15,7},{16,8},{17,9... | collective-permute-start | bytes 4718600 | tf_op jit(solution)/shard_map/ppermute | solution.py:10
  290.0 35.6 %copy-start.1 = (bf16[2048,384]{0,1:T(8,128)(2,1)S(1)}, bf16[2048,384]{0,1:T(8,128)(2,1)}, u32[]{:S(2)}) copy-start(bf16[2048,384]{0,1:T(8,128)(2,1)} %get-tuple-element.28) | copy-start | bytes 4718596
  290.0 35.6 %copy-start.7 = (f32[384]{0:T(512)S(1)}, f32[384]{0:T(512)}, u32[]{:S(2)}) copy-start(f32[384]{0:T(512)} %get-tuple-element.9) | copy-start | bytes 4612
  325.6 9.5 %copy-start.6 = (f32[384]{0:T(512)S(1)}, f32[384]{0:T(512)}, u32[]{:S(2)}) copy-start(f32[384]{0:T(512)} %get-tuple-element.5) | copy-start | bytes 4612
where the time goes:
time: 416 us; the launch traced here: 413 us
  waiting for transfers between devices  162 us (39%)
  matrix products  128 us (31%)
  starting transfers between devices  53.2 us (13%)
  blocking collectives  51.9 us (12%)
  local copies, waits for them, and re-layouts  10.4 us (2%)
  other arithmetic  6.2 us (1%)
    ppermute x8, waiting for transfers between devices, from_behind(): return lax.ppermute(block, axis, route)  162 us
    dot_general x4, matrix products, one_layer(): jnp.dot(hidden, proj_out, preferred_element_type=jnp.float32)  79.1 us
    ppermute x8, starting transfers between devices, from_behind(): return lax.ppermute(block, axis, route)  53.2 us
    all_to_all x1, blocking collectives, shards(): lax.all_to_all(state.T, 'seq', split_axis=0, concat_axis=1, tiled=True)  51.9 us
    dot_general x4, matrix products, one_layer(): pre = pre + jnp.dot(later, taps[2], preferred_element_type=jnp.float32)  39 us
  transfers between devices with their start and end apart: 8, of which 5 were waited for; matrix products, arithmetic and copies ran while one was open for 3% of the time, Pallas kernels for 0%

commit v1 on v0

v1 whole, which is shorter than its diff:
```python
import functools

import jax
import jax.numpy as jnp
import numpy as np
from jax import lax
from jax.experimental import pallas as pl
from jax.experimental.pallas import tpu as pltpu
from jax.sharding import PartitionSpec as P

AXIS = "seq"
ROWS = 16
VMEM_BYTES = 56 * 2**20


def rms_scale(wide, gain):
    inverse = lax.rsqrt(jnp.mean(wide * wide, axis=-1, keepdims=True) + 1e-06)
    return (wide * inverse * gain).astype(jnp.bfloat16)


def gelu(x):
    return (0.5 * x) * (1.0 + lax.erf(x * np.float32(np.sqrt(0.5))))


def dot(a, b):
    return jnp.dot(a, b, preferred_element_type=jnp.float32)


def tower_kernel(
    tile, unit, groups, x_ref, taps_ref, bias_ref, gain_conv_ref, gain_mlp_ref, in_ref, out_ref, pick_ref,
    y_ref, state_ref, normed_ref,
):
    layer = pl.program_id(0)
    layers = pl.num_programs(0)
    rows, channels = x_ref.shape
    pad = (normed_ref.shape[1] - rows) // 2
    now = lax.rem(layer, 2)

    @pl.when(layer == 0)
    def _():
        for slot in range(2):
            normed_ref[slot, :pad] = jnp.zeros((pad, channels), jnp.bfloat16)
            normed_ref[slot, pad + rows :] = jnp.zeros((pad, channels), jnp.bfloat16)
        for start in range(0, rows, tile):
            block = x_ref[start : start + tile]
            state_ref[start : start + tile] = block
            normed_ref[0, pad + start : pad + start + tile] = rms_scale(block.astype(jnp.float32), gain_conv_ref[0:1])

    shift = lax.shift_left(unit, layer)
    gain_next = gain_conv_ref[pl.ds(jnp.minimum(layer + 1, layers - 1), 1)]

    def step(i, carry):
        start = pl.multiple_of(i * tile, tile)
        base = pad + start
        near = [
            normed_ref[now, pl.ds(pl.multiple_of(base + offset, ROWS), tile)] for offset in (-shift, 0, shift)
        ]
        pre = dot(jnp.concatenate(near, axis=1), taps_ref[0]) + bias_ref[pl.ds(layer, 1)]
        wide = state_ref[pl.ds(start, tile)].astype(jnp.float32)
        middle = (wide + gelu(pre)).astype(jnp.bfloat16).astype(jnp.float32)
        inner = rms_scale(middle, gain_mlp_ref[pl.ds(layer, 1)])
        hidden = gelu(dot(inner, in_ref[0])).astype(jnp.bfloat16)
        new = (middle + dot(hidden, out_ref[0])).astype(jnp.bfloat16)
        state_ref[pl.ds(start, tile)] = new
        normed_ref[1 - now, pl.ds(pl.multiple_of(base, ROWS), tile)] = rms_scale(new.astype(jnp.float32), gain_next)
        return carry

    lax.fori_loop(0, rows // tile, step, 0)

    @pl.when(layer == layers - 1)
    def _():
        width = y_ref.shape[1] // groups
        for g in range(groups):
            part = state_ref[g * width : (g + 1) * width]
            if groups > 1:
                part = jnp.concatenate([part, state_ref[groups * width :]], axis=1)
            y_ref[:, g * width : (g + 1) * width] = lax.dot_general(
                pick_ref[g], part, (((1,), (1,)), ((), ())), preferred_element_type=jnp.float32
            ).astype(jnp.bfloat16)


def picker(channels, per, groups):
    if groups == 1:
        return np.eye(channels, dtype=np.float32)[None].astype(jnp.bfloat16)
    extra = per // groups
    pick = np.zeros((groups, channels // per * ROWS, 2 * channels), np.float32)
    for g in range(groups):
        for owner in range(channels // per):
            for r in range(per):
                pick[g, owner * ROWS + r, owner * per + r] = 1
            for r in range(extra):
                pick[g, owner * ROWS + per + r, channels + owner * per + g * extra + r] = 1
    return pick.astype(jnp.bfloat16)


def tower(x, conv_weight, conv_bias, conv_gain, mlp_gain, w_in, w_out, unit, per, groups):
    rows, channels = x.shape
    layers, _, hidden = w_in.shape
    pick = picker(channels, per, groups)
    out_shape = (pick.shape[1], rows // (groups + 1) * groups if groups > 1 else rows)
    pad = unit * 2 ** (layers - 1)
    tile = rows

    def whole(shape):
        return pl.BlockSpec(shape, lambda layer: (0,) * len(shape))

    def of_layer(*shape):
        return pl.BlockSpec((1, *shape), lambda layer: (layer, 0, 0))

    return pl.pallas_call(
        functools.partial(tower_kernel, tile, unit, groups),
        grid=(layers,),
        in_specs=[
            whole(x.shape),
            of_layer(3 * channels, channels),
            whole(conv_bias.shape),
            whole(conv_gain.shape),
            whole(mlp_gain.shape),
            of_layer(channels, hidden),
            of_layer(hidden, channels),
            whole(pick.shape),
        ],
        out_specs=whole(out_shape),
        out_shape=jax.ShapeDtypeStruct(out_shape, jnp.bfloat16),
        scratch_shapes=[
            pltpu.VMEM((rows, channels), jnp.bfloat16),
            pltpu.VMEM((2, rows + 2 * pad, channels), jnp.bfloat16),
        ],
        compiler_params=pltpu.CompilerParams(vmem_limit_bytes=VMEM_BYTES),
        name="tower",
    )(
        x,
        conv_weight.reshape(layers, 3 * channels, channels),
        conv_bias,
        conv_gain,
        mlp_gain,
        w_in,
        w_out,
        jnp.asarray(pick),
    )


def weave_kernel(per, groups, unit, x_ref, y_ref):
    sources, _, width = x_ref.shape
    extra, part = per // groups, width // groups
    block_rows = unit * sources

    def unpacked(source):
        rows = x_ref[source].astype(jnp.float32)
        rest = [rows[per : per + extra, g * part : (g + 1) * part] for g in range(groups)]
        return jnp.concatenate([rows[:per], jnp.concatenate(rest, axis=0)], axis=1)

    def step(pair, carry):
        even, odd = unpacked(2 * pair), unpacked(2 * pair + 1)
        low = lax.broadcasted_iota(jnp.int32, (per, 2 * unit), 1) < unit
        for m in range(sources // 2):
            cut = slice(2 * unit * m, 2 * unit * (m + 1))
            a, b = even[:, cut], odd[:, cut]
            for block, value in (
                (2 * m, jnp.where(low, a, pltpu.roll(b, unit, 1))),
                (2 * m + 1, jnp.where(low, pltpu.roll(a, unit, 1), b)),
            ):
                at = pl.multiple_of(block * block_rows + pair * 2 * unit, 2 * unit)
                y_ref[:, pl.ds(at, 2 * unit)] = value.astype(jnp.bfloat16)
        return carry

    lax.fori_loop(0, sources // 2, step, 0)


def weave(x, per, groups, unit, rows):
    sources = x.shape[0]
    return pl.pallas_call(
        functools.partial(weave_kernel, per, groups, unit),
        out_shape=jax.ShapeDtypeStruct((per, sources * rows), jnp.bfloat16),
        compiler_params=pltpu.CompilerParams(vmem_limit_bytes=VMEM_BYTES),
        name="weave",
    )(x)


def shards(activations, conv_weight, conv_bias, conv_gain, mlp_gain, w_in, w_out):
    devices = lax.axis_size(AXIS)
    rows, channels = activations.shape
    unit, per = rows // devices, channels // devices
    x = lax.all_to_all(activations, AXIS, split_axis=0, concat_axis=0, tiled=True)
    spare = ROWS - per
    groups = per // spare if 0 < spare < per and per % spare == 0 else 1
    fits = groups > 1 and 2 * unit == 128 and rows % ((groups + 1) * 128) == 0
    if not fits:
        groups = 1
    y = tower(x, conv_weight, conv_bias, conv_gain, mlp_gain, w_in, w_out, unit, per, groups)
    if fits:
        y = lax.all_to_all(y.reshape(devices, ROWS, -1), AXIS, split_axis=0, concat_axis=0, tiled=True)
        return weave(y, per, groups, unit, rows)
    y = lax.all_to_all(y.reshape(devices, per, rows), AXIS, split_axis=0, concat_axis=0, tiled=True)
    y = y.reshape(devices, per, devices, unit).transpose(1, 2, 0, 3)
    return y.reshape(per, devices * rows)


def solution(mesh):
    in_specs = (P(AXIS, None), P(), P(), P(), P(), P(), P())
    return jax.shard_map(shards, mesh=mesh, in_specs=in_specs, out_specs=P(AXIS, None), check_vma=False)
```

time: 416 us -> 127 us (0.31)
  waiting for transfers between devices: 162 us -> 0 us
  matrix products: 128 us -> 0 us
  starting transfers between devices: 53.2 us -> 0 us
  Pallas kernels: 0 us -> 39.8 us
  blocking collectives: 51.9 us -> 86.9 us
  local copies, waits for them, and re-layouts: 10.4 us -> 0 us
  other arithmetic: 6.2 us -> 0 us
    ppermute x8 -> x0, waiting for transfers between devices: 162 us -> none  [from_behind(): return lax.ppermute(block, axis, route)]
    dot_general x16 -> x0, matrix products: 128 us -> none  [the longest x4 79.1 us: one_layer(): jnp.dot(hidden, proj_out, preferred_element_type=jnp.float32)]
    ppermute x8 -> x0, starting transfers between devices: 53.2 us -> none  [from_behind(): return lax.ppermute(block, axis, route)]
    pallas_call x0 -> x2, Pallas kernels: none -> 39.8 us  [the longest x1 35.3 us: tower(): pl.pallas_call(functools.partial(tower_kernel, tile, unit, groups), grid=...]
    all_to_all x1 -> x2, blocking collectives: 51.9 us -> 86.9 us  [the longest x1 45.4 us: shards(): lax.all_to_all(activations, AXIS, split_axis=0, concat_axis=0, tiled=True)]
    convert_element_type x4 -> x0, other arithmetic: 5.81 us -> none  [rms_scale(): return (wide * inverse * gain[None, :]).astype(jnp.bfloat16)]
    unnamed x23 -> x0, local copies, waits for them, and re-layouts: 4.49 us -> none
  transfers between devices with their start and end apart: 8 -> 0, of which waited for: 5 -> 0; matrix products, arithmetic and copies ran while one was open for 3% -> 0% of each run, Pallas kernels for 0% -> 0%
where the time goes in v1:
time: 127 us
  blocking collectives  86.9 us (68%)
  Pallas kernels  39.8 us (31%)
    all_to_all x1, blocking collectives, shards(): lax.all_to_all(activations, AXIS, split_axis=0, concat_axis=0, tiled=True)  45.4 us
    all_to_all x1, blocking collectives, shards(): lax.all_to_all(y.reshape(devices, ROWS, -1), AXIS, split_axis=0, concat_a...  41.4 us
    pallas_call x1, Pallas kernels, tower(): pl.pallas_call(functools.partial(tower_kernel, tile, unit, groups), grid=...  35.3 us
    pallas_call x1, Pallas kernels, weave(): pl.pallas_call(functools.partial(weave_kernel, per, groups, unit), out_sh...  4.51 us

profile of v1, /device:TPU:0, one launch (start us, length us, event | category | flops | bytes accessed | tf_op | source)
XLA Modules:
  0.0 126.6 jit_solution(11893143347003352104)
XLA Ops:
  0.0 45.4 %all_to_all.16 = bf16[32,64,384]{2,1,0:T(8,128)(2,1)} all-to-all(bf16[32,64,384]{2,1,0:T(8,128)(2,1)} %bitcast.7), channel_id=1, replica_groups=mesh['seq'=32] {'seq'}, dimensions={0} | all-to-all | bytes 3145728 | tf_op jit(solution)/shard_map/all_to_all | solution.py:184
  45.4 35.3 %tower.1 = bf16[512,1536]{1,0:T(8,128)(2,1)} custom-call(bf16[2048,384]{1,0:T(8,128)(2,1)} %bitcast.5, bf16[4,1152,384]{2,1,0:T(8,128)(2,1)} %bitcast.6, f32[4,384]{1,0:T(4,128)} %bias_ref.1, f32[4,384]{1,0:T(4,128)} %gain_conv_ref.1, f32[4,384]{1,0:T(4,128)} %gain_mlp_ref.1, bf16[4,384,768]{2,1,0:T(8,128)(2,1)} %in_ref.1, bf16[4,768,384]{2,1,0:T(8,128)(2,1)} %out_ref.1, ...), custom_call_target="tpu_custom_call" | custom-call | tf_op jit(solution)/shard_map/tower/pallas_call | solution.py:110
  80.7 41.4 %all_to_all.17.x_ref = bf16[32,16,1536]{2,1,0:T(8,128)(2,1)} all-to-all(bf16[32,16,1536]{2,1,0:T(8,128)(2,1)} %bitcast.4), channel_id=1, replica_groups=mesh['seq'=32] {'seq'}, dimensions={0} | all-to-all | bytes 3145728 | tf_op jit(solution)/shard_map/all_to_all | solution.py:192
  122.1 4.5 %weave.1 = bf16[12,65536]{1,0:T(8,128)(2,1)} custom-call(bf16[32,16,1536]{2,1,0:T(8,128)(2,1)} %all_to_all.17.x_ref), custom_call_target="tpu_custom_call" | custom-call | tf_op jit(solution)/shard_map/weave/pallas_call | solution.py:172

commit v2 on v1

--- a/solution.py
+++ b/solution.py
@@ -9,6 +9,7 @@
 from jax.sharding import PartitionSpec as P
 
 AXIS = "seq"
+CHUNKS = 2
 ROWS = 16
 VMEM_BYTES = 56 * 2**20
 
@@ -126,6 +127,11 @@
             pltpu.VMEM((rows, channels), jnp.bfloat16),
             pltpu.VMEM((2, rows + 2 * pad, channels), jnp.bfloat16),
         ],
+        cost_estimate=pl.CostEstimate(
+            flops=2 * rows * conv_weight.size + 4 * rows * w_in.size,
+            bytes_accessed=2 * (conv_weight.size + 2 * w_in.size + 2 * x.size),
+            transcendentals=layers * rows * (channels + hidden),
+        ),
         compiler_params=pltpu.CompilerParams(vmem_limit_bytes=VMEM_BYTES),
         name="tower",
     )(
@@ -140,58 +146,102 @@
     )
 
 
-def weave_kernel(per, groups, unit, x_ref, y_ref):
+def weaver(units):
+    lanes = 128 // units
+    weave_of = np.zeros((lanes, lanes, units, lanes, lanes, units), np.float32)
+    for source in range(lanes):
+        for block in range(lanes):
+            weave_of[source, block, range(units), block, source, range(units)] = 1
+    return weave_of.reshape(lanes * 128, lanes * 128).astype(jnp.bfloat16)
+
+
+def weave_kernel(per, groups, unit, first, stride, x_ref, weave_ref, *refs):
+    y_ref, woven_ref, sems = refs[-3:]
     sources, _, width = x_ref.shape
     extra, part = per // groups, width // groups
-    block_rows = unit * sources
-
-    def unpacked(source):
-        rows = x_ref[source].astype(jnp.float32)
-        rest = [rows[per : per + extra, g * part : (g + 1) * part] for g in range(groups)]
-        return jnp.concatenate([rows[:per], jnp.concatenate(rest, axis=0)], axis=1)
-
-    def step(pair, carry):
-        even, odd = unpacked(2 * pair), unpacked(2 * pair + 1)
-        low = lax.broadcasted_iota(jnp.int32, (per, 2 * unit), 1) < unit
-        for m in range(sources // 2):
-            cut = slice(2 * unit * m, 2 * unit * (m + 1))
-            a, b = even[:, cut], odd[:, cut]
-            for block, value in (
-                (2 * m, jnp.where(low, a, pltpu.roll(b, unit, 1))),
-                (2 * m + 1, jnp.where(low, pltpu.roll(a, unit, 1), b)),
-            ):
-                at = pl.multiple_of(block * block_rows + pair * 2 * unit, 2 * unit)
-                y_ref[:, pl.ds(at, 2 * unit)] = value.astype(jnp.bfloat16)
-        return carry
-
-    lax.fori_loop(0, sources // 2, step, 0)
-
-
-def weave(x, per, groups, unit, rows):
+    span = unit * sources
+    lanes = 128 // unit
+    tiles = width // 128
+    part_tiles = part // 128
+    whole_blocks = tiles * lanes
+    for top in range(sources // lanes):
+        rows = [
+            jnp.concatenate(
+                [x_ref[top * lanes + source, :, t * 128 : (t + 1) * 128] for source in range(lanes)], axis=1
+            )
+            for t in range(tiles)
+        ]
+        swapped = dot(jnp.concatenate(rows, axis=0), weave_ref[...])
+
+        def piece(t, b, low, high):
+            return swapped[t * ROWS + low : t * ROWS + high, b * 128 : (b + 1) * 128]
+
+        for b in range(lanes):
+            for t in range(tiles):
+                at = (t * lanes + b) * span + top * 128
+                woven_ref[:, at : at + 128] = piece(t, b, 0, per).astype(jnp.bfloat16)
+            for t in range(part_tiles):
+                at = (whole_blocks + t * lanes + b) * span + top * 128
+                rest = [piece(g * part_tiles + t, b, per, per + extra) for g in range(groups)]
+                woven_ref[:, at : at + 128] = jnp.concatenate(rest, axis=0).astype(jnp.bfloat16)
+    copies = [
+        pltpu.make_async_copy(
+            woven_ref.at[:, pl.ds(block * span, span)],
+            y_ref.at[:, pl.ds(block * stride + first, span)],
+            sems.at[block],
+        )
+        for block in range(sources)
+    ]
+    for copy in copies:
+        copy.start()
+    for copy in copies:
+        copy.wait()
+
+
+def weave(x, y, per, groups, unit, first, stride):
     sources = x.shape[0]
+    vmem = pl.BlockSpec(memory_space=pltpu.VMEM)
+    operands = [x, jnp.asarray(weaver(unit))] + ([] if y is None else [y])
     return pl.pallas_call(
-        functools.partial(weave_kernel, per, groups, unit),
-        out_shape=jax.ShapeDtypeStruct((per, sources * rows), jnp.bfloat16),
+        functools.partial(weave_kernel, per, groups, unit, first, stride),
+        in_specs=[vmem, vmem] + ([] if y is None else [pl.BlockSpec(memory_space=pl.ANY)]),
+        out_specs=pl.BlockSpec(memory_space=pl.ANY),
+        out_shape=jax.ShapeDtypeStruct((per, sources * stride), jnp.bfloat16),
+        scratch_shapes=[
+            pltpu.VMEM((per, sources * unit * sources), jnp.bfloat16),
+            pltpu.SemaphoreType.DMA((sources,)),
+        ],
+        input_output_aliases={} if y is None else {2: 0},
         compiler_params=pltpu.CompilerParams(vmem_limit_bytes=VMEM_BYTES),
         name="weave",
-    )(x)
+    )(*operands)
+
+
+def exchange(x):
+    return lax.all_to_all(x, AXIS, split_axis=0, concat_axis=0, tiled=True)
 
 
 def shards(activations, conv_weight, conv_bias, conv_gain, mlp_gain, w_in, w_out):
     devices = lax.axis_size(AXIS)
     rows, channels = activations.shape
     unit, per = rows // devices, channels // devices
-    x = lax.all_to_all(activations, AXIS, split_axis=0, concat_axis=0, tiled=True)
+    weights = (conv_weight, conv_bias, conv_gain, mlp_gain, w_in, w_out)
     spare = ROWS - per
     groups = per // spare if 0 < spare < per and per % spare == 0 else 1
-    fits = groups > 1 and 2 * unit == 128 and rows % ((groups + 1) * 128) == 0
-    if not fits:
-        groups = 1
-    y = tower(x, conv_weight, conv_bias, conv_gain, mlp_gain, w_in, w_out, unit, per, groups)
-    if fits:
-        y = lax.all_to_all(y.reshape(devices, ROWS, -1), AXIS, split_axis=0, concat_axis=0, tiled=True)
-        return weave(y, per, groups, unit, rows)
-    y = lax.all_to_all(y.reshape(devices, per, rows), AXIS, split_axis=0, concat_axis=0, tiled=True)
+    part = unit // CHUNKS
+    if groups > 1 and part % ROWS == 0 and part * devices % ((groups + 1) * 128) == 0 and devices * part % 128 == 0:
+        size = rows // CHUNKS
+        y = None
+        towers = []
+        for c in range(CHUNKS):
+            x = exchange(activations[c * size : (c + 1) * size])
+            towers.append(tower(x, *weights, part, per, groups))
+        for c in range(CHUNKS):
+            x = exchange(towers[c].reshape(devices, ROWS, -1))
+            y = weave(x, y, per, groups, part, c * size, rows)
+        return y
+    y = tower(exchange(activations), *weights, unit, per, 1)
+    y = exchange(y.reshape(devices, per, rows))
     y = y.reshape(devices, per, devices, unit).transpose(1, 2, 0, 3)
     return y.reshape(per, devices * rows)
 

time: 127 us -> 111 us (0.87)
  blocking collectives: 86.9 us -> 27.8 us
  waiting for transfers between devices: 0 us -> 18.6 us
  starting transfers between devices: 0 us -> 13.9 us
  Pallas kernels: 39.8 us -> 46.6 us
  local copies, waits for them, and re-layouts: 0 us -> 3.29 us
    all_to_all x2 -> x1, blocking collectives: 86.9 us -> 27.8 us  [exchange(): return lax.all_to_all(x, AXIS, split_axis=0, concat_axis=0, tiled=True)]
    all_to_all x0 -> x3, waiting for transfers between devices: none -> 18.6 us  [exchange(): return lax.all_to_all(x, AXIS, split_axis=0, concat_axis=0, tiled=True)]
    all_to_all x0 -> x3, starting transfers between devices: none -> 13.9 us  [exchange(): return lax.all_to_all(x, AXIS, split_axis=0, concat_axis=0, tiled=True)]
    pallas_call x1 -> x2, Pallas kernels: 35.3 us -> 39.8 us  [tower(): pl.pallas_call(functools.partial(tower_kernel, tile, unit, groups), grid=...]
    slice x0 -> x1, local copies, waits for them, and re-layouts: none -> 2.41 us  [shards(): x = exchange(activations[c * size:(c + 1) * size])]
    pallas_call x1 -> x2, Pallas kernels: 4.51 us -> 6.79 us  [weave(): pl.pallas_call(functools.partial(weave_kernel, per, groups, unit, first,...]
  transfers between devices with their start and end apart: 0 -> 3, of which waited for: 0 -> 3; matrix products, arithmetic and copies ran while one was open for 0% -> 0% of each run, Pallas kernels for 0% -> 39%
where the time goes in v2:
time: 111 us; the launch traced here: 110 us
  Pallas kernels  46.6 us (42%)
  blocking collectives  27.8 us (25%)
  waiting for transfers between devices  18.6 us (17%)
  starting transfers between devices  13.9 us (13%)
  local copies, waits for them, and re-layouts  3.29 us (3%)
    pallas_call x2, Pallas kernels, tower(): pl.pallas_call(functools.partial(tower_kernel, tile, unit, groups), grid=...  39.8 us
    all_to_all x1, blocking collectives, exchange(): return lax.all_to_all(x, AXIS, split_axis=0, concat_axis=0, tiled=True)  27.8 us
    all_to_all x3, waiting for transfers between devices, exchange(): return lax.all_to_all(x, AXIS, split_axis=0, concat_axis=0, tiled=True)  18.6 us
    all_to_all x3, starting transfers between devices, exchange(): return lax.all_to_all(x, AXIS, split_axis=0, concat_axis=0, tiled=True)  13.9 us
    pallas_call x2, Pallas kernels, weave(): pl.pallas_call(functools.partial(weave_kernel, per, groups, unit, first,...  6.79 us
    slice x1, local copies, waits for them, and re-layouts, shards(): x = exchange(activations[c * size:(c + 1) * size])  2.41 us
  transfers between devices with their start and end apart: 3, of which 3 were waited for; matrix products, arithmetic and copies ran while one was open for 0% of the time, Pallas kernels for 39%

profile of v2, /device:TPU:0, one launch (start us, length us, event | category | flops | bytes accessed | tf_op | source)
XLA Modules:
  0.0 110.3 jit_solution(13754850450857865574)
XLA Ops:
  0.0 2.4 %fusion = (bf16[1024,384]{1,0:T(8,128)(2,1)S(1)}, bf16[1024,384]{1,0:T(8,128)(2,1)}) fusion(bf16[2048,384]{1,0:T(8,128)(2,1)} %param.11), kind=kLoop, calls=%fused_computation | loop fusion | bytes 3145728 | tf_op jit(solution)/shard_map/slice | solution.py:237
  2.4 27.8 %all_to_all.32 = bf16[32,32,384]{2,1,0:T(8,128)(2,1)} all-to-all(bf16[32,32,384]{2,1,0:T(8,128)(2,1)S(1)} %bitcast.7), channel_id=1, replica_groups=mesh['seq'=32] {'seq'}, dimensions={0} | all-to-all | bytes 1572864 | tf_op jit(solution)/shard_map/all_to_all | solution.py:221
  30.2 3.6 %all-to-all-start = ((bf16[32,32,384]{2,1,0:T(8,128)(2,1)}), bf16[32,32,384]{2,1,0:T(8,128)(2,1)S(1)}, u32[]{:S(2)}, u32[]{:S(2)}) async-start(bf16[32,32,384]{2,1,0:T(8,128)(2,1)} %bitcast), calls=%async_computation | async-start | bytes 1572864 | tf_op jit(solution)/shard_map/all_to_all | solution.py:221
  33.9 19.9 %tower.3 = bf16[512,768]{1,0:T(8,128)(2,1)} custom-call(bf16[1024,384]{1,0:T(8,128)(2,1)} %bitcast.11, bf16[4,1152,384]{2,1,0:T(8,128)(2,1)} %bitcast.12, f32[4,384]{1,0:T(4,128)} %bias_ref.3, f32[4,384]{1,0:T(4,128)} %gain_conv_ref.3, f32[4,384]{1,0:T(4,128)} %gain_mlp_ref.3, bf16[4,384,768]{2,1,0:T(8,128)(2,1)} %in_ref.3, bf16[4,768,384]{2,1,0:T(8,128)(2,1)} %out_ref.3, ...), custom_call_target="tpu_custom_call" | custom-call | flops 8455716864 | bytes 9830400 | tf_op jit(solution)/shard_map/tower/pallas_call | solution.py:111
  53.8 0.7 all-to-all-done
  54.5 0.0 copy-start.2
  54.5 5.2 %all-to-all-start.3 = ((bf16[32,16,768]{2,1,0:T(8,128)(2,1)}), bf16[32,16,768]{2,1,0:T(8,128)(2,1)S(1)}, u32[]{:S(2)}, u32[]{:S(2)}) async-start(bf16[32,16,768]{2,1,0:T(8,128)(2,1)} %bitcast.9), calls=%async_computation.3 | async-start | bytes 1572864 | tf_op jit(solution)/shard_map/all_to_all | solution.py:221
  59.6 0.0 copy-done.2
  59.6 19.9 %tower.2 = bf16[512,768]{1,0:T(8,128)(2,1)} custom-call(bf16[1024,384]{1,0:T(8,128)(2,1)} %bitcast.8, bf16[4,1152,384]{2,1,0:T(8,128)(2,1)} %bitcast.13, f32[4,384]{1,0:T(4,128)} %bias_ref.3, f32[4,384]{1,0:T(4,128)} %gain_conv_ref.3, f32[4,384]{1,0:T(4,128)} %gain_mlp_ref.3, bf16[4,384,768]{2,1,0:T(8,128)(2,1)} %in_ref.3, bf16[4,768,384]{2,1,0:T(8,128)(2,1)} %out_ref.3, ...), custom_call_target="tpu_custom_call" | custom-call | flops 8455716864 | bytes 9830400 | tf_op jit(solution)/shard_map/tower/pallas_call | solution.py:111
  79.5 0.7 all-to-all-done.3.x_ref
  80.3 0.0 copy-start
  80.3 5.1 %all-to-all-start.1 = ((bf16[32,16,768]{2,1,0:T(8,128)(2,1)}), bf16[32,16,768]{2,1,0:T(8,128)(2,1)S(1)}, u32[]{:S(2)}, u32[]{:S(2)}) async-start(bf16[32,16,768]{2,1,0:T(8,128)(2,1)} %bitcast.10), calls=%async_computation.1 | async-start | bytes 1572864 | tf_op jit(solution)/shard_map/all_to_all | solution.py:221
  85.4 0.0 copy-done
  85.4 3.4 %weave.2.refs_0_ = bf16[12,65536]{1,0:T(8,128)(2,1)} custom-call(bf16[32,16,768]{2,1,0:T(8,128)(2,1)} %copy-done, bf16[512,512]{1,0:T(8,128)(2,1)} %constant.5.clone.weave_ref), custom_call_target="tpu_custom_call" | custom-call | tf_op jit(solution)/shard_map/weave/pallas_call | solution.py:205
  88.8 17.2 %all-to-all-done.1.x_ref = bf16[32,16,768]{2,1,0:T(8,128)(2,1)S(1)} async-done(((bf16[32,16,768]{2,1,0:T(8,128)(2,1)}), bf16[32,16,768]{2,1,0:T(8,128)(2,1)S(1)}, u32[]{:S(2)}, u32[]{:S(2)}) %all-to-all-start.1) | async-done | bytes 786464 | tf_op jit(solution)/shard_map/all_to_all | solution.py:221
  106.0 0.0 copy-start.1
  106.0 0.9 copy-done.1
  106.9 3.4 %weave.3 = bf16[12,65536]{1,0:T(8,128)(2,1)} custom-call(bf16[32,16,768]{2,1,0:T(8,128)(2,1)} %copy-done.1, bf16[512,512]{1,0:T(8,128)(2,1)} %constant.5.clone.weave_ref, bf16[12,65536]{1,0:T(8,128)(2,1)} %weave.2.refs_0_), custom_call_target="tpu_custom_call", output_to_operand_aliasing={{}: (2, {})} | custom-call | tf_op jit(solution)/shard_map/weave/pallas_call | solution.py:205
Async XLA Ops:
  30.2 24.2 %all-to-all-start = ((bf16[32,32,384]{2,1,0:T(8,128)(2,1)}), bf16[32,32,384]{2,1,0:T(8,128)(2,1)S(1)}, u32[]{:S(2)}, u32[]{:S(2)}) async-start(bf16[32,32,384]{2,1,0:T(8,128)(2,1)} %bitcast), calls=%async_computation | async-start | bytes 1572864 | tf_op jit(solution)/shard_map/all_to_all | solution.py:221
  54.5 5.2 %copy-start.2 = (bf16[32,32,384]{2,1,0:T(8,128)(2,1)}, bf16[32,32,384]{2,1,0:T(8,128)(2,1)S(1)}, u32[]{:S(2)}) copy-start(bf16[32,32,384]{2,1,0:T(8,128)(2,1)S(1)} %all-to-all-done) | copy-start | bytes 2359300
  54.5 25.8 %all-to-all-start.3 = ((bf16[32,16,768]{2,1,0:T(8,128)(2,1)}), bf16[32,16,768]{2,1,0:T(8,128)(2,1)S(1)}, u32[]{:S(2)}, u32[]{:S(2)}) async-start(bf16[32,16,768]{2,1,0:T(8,128)(2,1)} %bitcast.9), calls=%async_computation.3 | async-start | bytes 1572864 | tf_op jit(solution)/shard_map/all_to_all | solution.py:221
  80.3 5.1 %copy-start = (bf16[32,16,768]{2,1,0:T(8,128)(2,1)}, bf16[32,16,768]{2,1,0:T(8,128)(2,1)S(1)}, u32[]{:S(2)}) copy-start(bf16[32,16,768]{2,1,0:T(8,128)(2,1)S(1)} %all-to-all-done.3.x_ref) | copy-start | bytes 2359300
  80.3 25.8 %all-to-all-start.1 = ((bf16[32,16,768]{2,1,0:T(8,128)(2,1)}), bf16[32,16,768]{2,1,0:T(8,128)(2,1)S(1)}, u32[]{:S(2)}, u32[]{:S(2)}) async-start(bf16[32,16,768]{2,1,0:T(8,128)(2,1)} %bitcast.10), calls=%async_computation.1 | async-start | bytes 1572864 | tf_op jit(solution)/shard_map/all_to_all | solution.py:221
  106.0 0.9 copy-start.1

commit v3 on v2

--- a/solution.py
+++ b/solution.py
@@ -10,8 +10,8 @@
 
 AXIS = "seq"
 CHUNKS = 2
+TILE = 256
 ROWS = 16
-VMEM_BYTES = 56 * 2**20
 
 
 def rms_scale(wide, gain):
@@ -50,23 +50,26 @@
     shift = lax.shift_left(unit, layer)
     gain_next = gain_conv_ref[pl.ds(jnp.minimum(layer + 1, layers - 1), 1)]
 
-    def step(i, carry):
-        start = pl.multiple_of(i * tile, tile)
-        base = pad + start
+    bias, gain_mlp = bias_ref[pl.ds(layer, 1)], gain_mlp_ref[pl.ds(layer, 1)]
+    starts = range(0, rows, tile)
+
+    def mixed(start):
         near = [
-            normed_ref[now, pl.ds(pl.multiple_of(base + offset, ROWS), tile)] for offset in (-shift, 0, shift)
+            normed_ref[now, pl.ds(pl.multiple_of(pad + start + offset, ROWS), tile)] for offset in (-shift, 0, shift)
         ]
-        pre = dot(jnp.concatenate(near, axis=1), taps_ref[0]) + bias_ref[pl.ds(layer, 1)]
-        wide = state_ref[pl.ds(start, tile)].astype(jnp.float32)
-        middle = (wide + gelu(pre)).astype(jnp.bfloat16).astype(jnp.float32)
-        inner = rms_scale(middle, gain_mlp_ref[pl.ds(layer, 1)])
-        hidden = gelu(dot(inner, in_ref[0])).astype(jnp.bfloat16)
-        new = (middle + dot(hidden, out_ref[0])).astype(jnp.bfloat16)
-        state_ref[pl.ds(start, tile)] = new
-        normed_ref[1 - now, pl.ds(pl.multiple_of(base, ROWS), tile)] = rms_scale(new.astype(jnp.float32), gain_next)
-        return carry
-
-    lax.fori_loop(0, rows // tile, step, 0)
+        pre = dot(jnp.concatenate(near, axis=1), taps_ref[0]) + bias
+        return (state_ref[start : start + tile].astype(jnp.float32) + gelu(pre)).astype(jnp.bfloat16)
+
+    def widened(middle):
+        inner = rms_scale(middle.astype(jnp.float32), gain_mlp)
+        return gelu(dot(inner, in_ref[0])).astype(jnp.bfloat16)
+
+    middles = [mixed(start) for start in starts]
+    hiddens = [widened(middle) for middle in middles]
+    for start, middle, hidden in zip(starts, middles, hiddens):
+        new = (middle.astype(jnp.float32) + dot(hidden, out_ref[0])).astype(jnp.bfloat16)
+        state_ref[start : start + tile] = new
+        normed_ref[1 - now, pad + start : pad + start + tile] = rms_scale(new.astype(jnp.float32), gain_next)
 
     @pl.when(layer == layers - 1)
     def _():
@@ -100,7 +103,7 @@
     pick = picker(channels, per, groups)
     out_shape = (pick.shape[1], rows // (groups + 1) * groups if groups > 1 else rows)
     pad = unit * 2 ** (layers - 1)
-    tile = rows
+    tile = TILE if rows % TILE == 0 else rows
 
     def whole(shape):
         return pl.BlockSpec(shape, lambda layer: (0,) * len(shape))
@@ -132,7 +135,7 @@
             bytes_accessed=2 * (conv_weight.size + 2 * w_in.size + 2 * x.size),
             transcendentals=layers * rows * (channels + hidden),
         ),
-        compiler_params=pltpu.CompilerParams(vmem_limit_bytes=VMEM_BYTES),
+        compiler_params=pltpu.CompilerParams(vmem_limit_bytes=56 * 2**20),
         name="tower",
     )(
         x,
@@ -161,29 +164,7 @@
     extra, part = per // groups, width // groups
     span = unit * sources
     lanes = 128 // unit
-    tiles = width // 128
-    part_tiles = part // 128
-    whole_blocks = tiles * lanes
-    for top in range(sources // lanes):
-        rows = [
-            jnp.concatenate(
-                [x_ref[top * lanes + source, :, t * 128 : (t + 1) * 128] for source in range(lanes)], axis=1
-            )
-            for t in range(tiles)
-        ]
-        swapped = dot(jnp.concatenate(rows, axis=0), weave_ref[...])
-
-        def piece(t, b, low, high):
-            return swapped[t * ROWS + low : t * ROWS + high, b * 128 : (b + 1) * 128]
-
-        for b in range(lanes):
-            for t in range(tiles):
-                at = (t * lanes + b) * span + top * 128
-                woven_ref[:, at : at + 128] = piece(t, b, 0, per).astype(jnp.bfloat16)
-            for t in range(part_tiles):
-                at = (whole_blocks + t * lanes + b) * span + top * 128
-                rest = [piece(g * part_tiles + t, b, per, per + extra) for g in range(groups)]
-                woven_ref[:, at : at + 128] = jnp.concatenate(rest, axis=0).astype(jnp.bfloat16)
+    tops, tiles, part_tiles = sources // lanes, width // 128, part // 128
     copies = [
         pltpu.make_async_copy(
             woven_ref.at[:, pl.ds(block * span, span)],
@@ -192,27 +173,53 @@
         )
         for block in range(sources)
     ]
-    for copy in copies:
-        copy.start()
+
+    def put(block, top, value):
+        at = block * span + top * 128
+        woven_ref[:, at : at + 128] = value.astype(jnp.bfloat16)
+
+    swapped = []
+    for t in range(tiles):
+        cut = slice(t * 128, (t + 1) * 128)
+        rows = [
+            jnp.concatenate([x_ref[top * lanes + source, :, cut] for source in range(lanes)], axis=1)
+            for top in range(tops)
+        ]
+        swapped.append(dot(jnp.concatenate(rows, axis=0), weave_ref[...]))
+        for b in range(lanes):
+            for top in range(tops):
+                low = top * ROWS
+                put(t * lanes + b, top, swapped[t][low : low + per, b * 128 : (b + 1) * 128])
+            copies[t * lanes + b].start()
+    for t in range(part_tiles):
+        for b in range(lanes):
+            block = (tiles + t) * lanes + b
+            for top in range(tops):
+                low = top * ROWS + per
+                rest = [
+                    swapped[g * part_tiles + t][low : low + extra, b * 128 : (b + 1) * 128] for g in range(groups)
+                ]
+                put(block, top, jnp.concatenate(rest, axis=0))
+            copies[block].start()
     for copy in copies:
         copy.wait()
 
 
 def weave(x, y, per, groups, unit, first, stride):
     sources = x.shape[0]
-    vmem = pl.BlockSpec(memory_space=pltpu.VMEM)
+    vmem, anywhere = pl.BlockSpec(memory_space=pltpu.VMEM), pl.BlockSpec(memory_space=pl.ANY)
     operands = [x, jnp.asarray(weaver(unit))] + ([] if y is None else [y])
     return pl.pallas_call(
         functools.partial(weave_kernel, per, groups, unit, first, stride),
-        in_specs=[vmem, vmem] + ([] if y is None else [pl.BlockSpec(memory_space=pl.ANY)]),
-        out_specs=pl.BlockSpec(memory_space=pl.ANY),
+        in_specs=[vmem, vmem] + ([] if y is None else [anywhere]),
+        out_specs=anywhere,
         out_shape=jax.ShapeDtypeStruct((per, sources * stride), jnp.bfloat16),
         scratch_shapes=[
             pltpu.VMEM((per, sources * unit * sources), jnp.bfloat16),
             pltpu.SemaphoreType.DMA((sources,)),
         ],
         input_output_aliases={} if y is None else {2: 0},
-        compiler_params=pltpu.CompilerParams(vmem_limit_bytes=VMEM_BYTES),
+        compiler_params=pltpu.CompilerParams(vmem_limit_bytes=12 * 2**20),
         name="weave",
     )(*operands)
 
@@ -234,7 +241,8 @@
         y = None
         towers = []
         for c in range(CHUNKS):
-            x = exchange(activations[c * size : (c + 1) * size])
+            whole = activations if c == 0 else lax.optimization_barrier(activations)
+            x = exchange(whole[c * size : (c + 1) * size])
             towers.append(tower(x, *weights, part, per, groups))
         for c in range(CHUNKS):
             x = exchange(towers[c].reshape(devices, ROWS, -1))

time: 111 us -> 105 us (0.946)
  blocking collectives: 27.8 us -> 0 us
  waiting for transfers between devices: 18.6 us -> 43.5 us
  Pallas kernels: 46.6 us -> 39.5 us
  starting transfers between devices: 13.9 us -> 18.2 us
    all_to_all x1 -> x0, blocking collectives: 27.8 us -> none  [exchange(): return lax.all_to_all(x, AXIS, split_axis=0, concat_axis=0, tiled=True)]
    all_to_all x3 -> x4, waiting for transfers between devices: 18.6 us -> 43.5 us  [exchange(): return lax.all_to_all(x, AXIS, split_axis=0, concat_axis=0, tiled=True)]
    all_to_all x3 -> x4, starting transfers between devices: 13.9 us -> 18.2 us  [exchange(): return lax.all_to_all(x, AXIS, split_axis=0, concat_axis=0, tiled=True)]
    pallas_call x2, Pallas kernels: 6.79 us -> 3.21 us  [weave(): pl.pallas_call(functools.partial(weave_kernel, per, groups, unit, first,...]
    pallas_call x2, Pallas kernels: 39.8 us -> 36.3 us  [tower(): pl.pallas_call(functools.partial(tower_kernel, tile, unit, groups), grid=...]
    slice x1 -> x2, local copies, waits for them, and re-layouts: 2.41 us -> 3.18 us  [shards(): x = exchange(whole[c * size:(c + 1) * size])]
  transfers between devices with their start and end apart: 3 -> 4, of which waited for: 3 -> 4; matrix products, arithmetic and copies ran while one was open for 0% -> 1% of each run, Pallas kernels for 39% -> 36%
where the time goes in v3:
time: 105 us; the launch traced here: 104 us
  waiting for transfers between devices  43.5 us (41%)
  Pallas kernels  39.5 us (38%)
  starting transfers between devices  18.2 us (17%)
  local copies, waits for them, and re-layouts  3.2 us (3%)
    all_to_all x4, waiting for transfers between devices, exchange(): return lax.all_to_all(x, AXIS, split_axis=0, concat_axis=0, tiled=True)  43.5 us
    pallas_call x2, Pallas kernels, tower(): pl.pallas_call(functools.partial(tower_kernel, tile, unit, groups), grid=...  36.3 us
    all_to_all x4, starting transfers between devices, exchange(): return lax.all_to_all(x, AXIS, split_axis=0, concat_axis=0, tiled=True)  18.2 us
    pallas_call x2, Pallas kernels, weave(): pl.pallas_call(functools.partial(weave_kernel, per, groups, unit, first,...  3.21 us
    slice x2, local copies, waits for them, and re-layouts, shards(): x = exchange(whole[c * size:(c + 1) * size])  3.18 us
  transfers between devices with their start and end apart: 4, of which 4 were waited for; matrix products, arithmetic and copies ran while one was open for 1% of the time, Pallas kernels for 36%

profile of v3, /device:TPU:0, one launch (start us, length us, event | category | flops | bytes accessed | tf_op | source)
XLA Modules:
  0.0 104.5 jit_solution(14615453577042062250)
XLA Ops:
  0.0 0.0 copy-start.1
  0.0 2.2 %slice.7 = bf16[1024,384]{1,0:T(8,128)(2,1)} slice(bf16[2048,384]{1,0:T(8,128)(2,1)} %param.11), slice={[0:1024], [0:384]} | slice | bytes 1572864 | tf_op jit(solution)/shard_map/slice | solution.py:245
  2.2 7.3 %all-to-all-start.2 = ((bf16[32,32,384]{2,1,0:T(8,128)(2,1)}), bf16[32,32,384]{2,1,0:T(8,128)(2,1)S(1)}, u32[]{:S(2)}, u32[]{:S(2)}) async-start(bf16[32,32,384]{2,1,0:T(8,128)(2,1)} %bitcast.4), calls=%async_computation.2 | async-start | bytes 1572864 | tf_op jit(solution)/shard_map/all_to_all | solution.py:228
  9.5 0.0 copy-done.1
  9.5 1.0 slice.8
  10.5 19.6 %all-to-all-done.2 = bf16[32,32,384]{2,1,0:T(8,128)(2,1)S(1)} async-done(((bf16[32,32,384]{2,1,0:T(8,128)(2,1)}), bf16[32,32,384]{2,1,0:T(8,128)(2,1)S(1)}, u32[]{:S(2)}, u32[]{:S(2)}) %all-to-all-start.2) | async-done | bytes 786464 | tf_op jit(solution)/shard_map/all_to_all | solution.py:228
  30.1 0.0 copy-start.3
  30.1 3.6 %all-to-all-start = ((bf16[32,32,384]{2,1,0:T(8,128)(2,1)}), bf16[32,32,384]{2,1,0:T(8,128)(2,1)S(1)}, u32[]{:S(2)}, u32[]{:S(2)}) async-start(bf16[32,32,384]{2,1,0:T(8,128)(2,1)} %bitcast), calls=%async_computation | async-start | bytes 1572864 | tf_op jit(solution)/shard_map/all_to_all | solution.py:228
  33.8 0.0 copy-done.3
  33.8 18.1 %tower.3 = bf16[512,768]{1,0:T(8,128)(2,1)} custom-call(bf16[1024,384]{1,0:T(8,128)(2,1)} %bitcast.8, bf16[4,1152,384]{2,1,0:T(8,128)(2,1)} %bitcast.11, f32[4,384]{1,0:T(4,128)} %bias_ref.3, f32[4,384]{1,0:T(4,128)} %gain_conv_ref.3, f32[4,384]{1,0:T(4,128)} %gain_mlp_ref.3, bf16[4,384,768]{2,1,0:T(8,128)(2,1)} %in_ref.3, bf16[4,768,384]{2,1,0:T(8,128)(2,1)} %out_ref.3, ...), custom_call_target="tpu_custom_call" | custom-call | flops 8455716864 | bytes 9830400 | tf_op jit(solution)/shard_map/tower/pallas_call | solution.py:114
  51.9 2.5 %all-to-all-done = bf16[32,32,384]{2,1,0:T(8,128)(2,1)S(1)} async-done(((bf16[32,32,384]{2,1,0:T(8,128)(2,1)}), bf16[32,32,384]{2,1,0:T(8,128)(2,1)S(1)}, u32[]{:S(2)}, u32[]{:S(2)}) %all-to-all-start) | async-done | bytes 786464 | tf_op jit(solution)/shard_map/all_to_all | solution.py:228
  54.4 0.0 copy-start.2
  54.4 3.6 %all-to-all-start.3 = ((bf16[32,16,768]{2,1,0:T(8,128)(2,1)}), bf16[32,16,768]{2,1,0:T(8,128)(2,1)S(1)}, u32[]{:S(2)}, u32[]{:S(2)}) async-start(bf16[32,16,768]{2,1,0:T(8,128)(2,1)} %bitcast.9), calls=%async_computation.3 | async-start | bytes 1572864 | tf_op jit(solution)/shard_map/all_to_all | solution.py:228
  58.0 0.0 copy-done.2
  58.0 0.0 copy-start
  58.0 18.2 %tower.2 = bf16[512,768]{1,0:T(8,128)(2,1)} custom-call(bf16[1024,384]{1,0:T(8,128)(2,1)} %bitcast.7, bf16[4,1152,384]{2,1,0:T(8,128)(2,1)} %bitcast.12, f32[4,384]{1,0:T(4,128)} %bias_ref.3, f32[4,384]{1,0:T(4,128)} %gain_conv_ref.3, f32[4,384]{1,0:T(4,128)} %gain_mlp_ref.3, bf16[4,384,768]{2,1,0:T(8,128)(2,1)} %in_ref.3, bf16[4,768,384]{2,1,0:T(8,128)(2,1)} %out_ref.3, ...), custom_call_target="tpu_custom_call" | custom-call | flops 8455716864 | bytes 9830400 | tf_op jit(solution)/shard_map/tower/pallas_call | solution.py:114
  76.2 2.4 %all-to-all-done.3.x_ref = bf16[32,16,768]{2,1,0:T(8,128)(2,1)S(1)} async-done(((bf16[32,16,768]{2,1,0:T(8,128)(2,1)}), bf16[32,16,768]{2,1,0:T(8,128)(2,1)S(1)}, u32[]{:S(2)}, u32[]{:S(2)}) %all-to-all-start.3) | async-done | bytes 786464 | tf_op jit(solution)/shard_map/all_to_all | solution.py:228
  78.6 3.6 %all-to-all-start.1 = ((bf16[32,16,768]{2,1,0:T(8,128)(2,1)}), bf16[32,16,768]{2,1,0:T(8,128)(2,1)S(1)}, u32[]{:S(2)}, u32[]{:S(2)}) async-start(bf16[32,16,768]{2,1,0:T(8,128)(2,1)} %bitcast.10), calls=%async_computation.1 | async-start | bytes 1572864 | tf_op jit(solution)/shard_map/all_to_all | solution.py:228
  82.3 0.0 copy-done
  82.3 1.6 %weave.2.refs_0_ = bf16[12,65536]{1,0:T(8,128)(2,1)} custom-call(bf16[32,16,768]{2,1,0:T(8,128)(2,1)S(1)} %all-to-all-done.3.x_ref, bf16[512,512]{1,0:T(8,128)(2,1)S(1)} %copy-done), custom_call_target="tpu_custom_call" | custom-call | tf_op jit(solution)/shard_map/weave/pallas_call | solution.py:212
  83.9 19.0 %all-to-all-done.1.x_ref = bf16[32,16,768]{2,1,0:T(8,128)(2,1)S(1)} async-done(((bf16[32,16,768]{2,1,0:T(8,128)(2,1)}), bf16[32,16,768]{2,1,0:T(8,128)(2,1)S(1)}, u32[]{:S(2)}, u32[]{:S(2)}) %all-to-all-start.1) | async-done | bytes 786464 | tf_op jit(solution)/shard_map/all_to_all | solution.py:228
  102.9 1.6 %weave.3 = bf16[12,65536]{1,0:T(8,128)(2,1)} custom-call(bf16[32,16,768]{2,1,0:T(8,128)(2,1)S(1)} %all-to-all-done.1.x_ref, bf16[512,512]{1,0:T(8,128)(2,1)S(1)} %copy-done, bf16[12,65536]{1,0:T(8,128)(2,1)} %weave.2.refs_0_), custom_call_target="tpu_custom_call", output_to_operand_aliasing={{}: (2, {})} | custom-call | tf_op jit(solution)/shard_map/weave/pallas_call | solution.py:212
Async XLA Ops:
  0.0 9.5 %copy-start.1 = (bf16[2048,384]{1,0:T(8,128)(2,1)S(1)}, bf16[2048,384]{1,0:T(8,128)(2,1)}, u32[]{:S(2)}) copy-start(bf16[2048,384]{1,0:T(8,128)(2,1)} %param.11) | copy-start | bytes 4718596
  2.2 27.9 %all-to-all-start.2 = ((bf16[32,32,384]{2,1,0:T(8,128)(2,1)}), bf16[32,32,384]{2,1,0:T(8,128)(2,1)S(1)}, u32[]{:S(2)}, u32[]{:S(2)}) async-start(bf16[32,32,384]{2,1,0:T(8,128)(2,1)} %bitcast.4), calls=%async_computation.2 | async-start | bytes 1572864 | tf_op jit(solution)/shard_map/all_to_all | solution.py:228
  30.1 3.6 %copy-start.3 = (bf16[32,32,384]{2,1,0:T(8,128)(2,1)}, bf16[32,32,384]{2,1,0:T(8,128)(2,1)S(1)}, u32[]{:S(2)}) copy-start(bf16[32,32,384]{2,1,0:T(8,128)(2,1)S(1)} %all-to-all-done.2) | copy-start | bytes 2359300
  30.1 24.2 %all-to-all-start = ((bf16[32,32,384]{2,1,0:T(8,128)(2,1)}), bf16[32,32,384]{2,1,0:T(8,128)(2,1)S(1)}, u32[]{:S(2)}, u32[]{:S(2)}) async-start(bf16[32,32,384]{2,1,0:T(8,128)(2,1)} %bitcast), calls=%async_computation | async-start | bytes 1572864 | tf_op jit(solution)/shard_map/all_to_all | solution.py:228
  54.4 3.6 %copy-start.2 = (bf16[32,32,384]{2,1,0:T(8,128)(2,1)}, bf16[32,32,384]{2,1,0:T(8,128)(2,1)S(1)}, u32[]{:S(2)}) copy-start(bf16[32,32,384]{2,1,0:T(8,128)(2,1)S(1)} %all-to-all-done) | copy-start | bytes 2359300
  54.4 24.2 %all-to-all-start.3 = ((bf16[32,16,768]{2,1,0:T(8,128)(2,1)}), bf16[32,16,768]{2,1,0:T(8,128)(2,1)S(1)}, u32[]{:S(2)}, u32[]{:S(2)}) async-start(bf16[32,16,768]{2,1,0:T(8,128)(2,1)} %bitcast.9), calls=%async_computation.3 | async-start | bytes 1572864 | tf_op jit(solution)/shard_map/all_to_all | solution.py:228
  58.0 24.2 %copy-start = (bf16[512,512]{1,0:T(8,128)(2,1)S(1)}, bf16[512,512]{1,0:T(8,128)(2,1)}, u32[]{:S(2)}) copy-start(bf16[512,512]{1,0:T(8,128)(2,1)} %constant.5.clone.weave_ref) | copy-start | bytes 1572868
  78.6 24.2 %all-to-all-start.1 = ((bf16[32,16,768]{2,1,0:T(8,128)(2,1)}), bf16[32,16,768]{2,1,0:T(8,128)(2,1)S(1)}, u32[]{:S(2)}, u32[]{:S(2)}) async-start(bf16[32,16,768]{2,1,0:T(8,128)(2,1)} %bitcast.10), calls=%async_computation.1 | async-start | bytes 1572864 | tf_op jit(solution)/shard_map/all_to_all | solution.py:228

commit v4 on v3

--- a/solution.py
+++ b/solution.py
@@ -10,6 +10,8 @@
 
 AXIS = "seq"
 CHUNKS = 2
+TIE = 1
+STAGES = ((3, 2), (1, 2), (0, 1))
 TILE = 256
 ROWS = 16
 
@@ -28,12 +30,13 @@
 
 
 def tower_kernel(
-    tile, unit, groups, x_ref, taps_ref, bias_ref, gain_conv_ref, gain_mlp_ref, in_ref, out_ref, pick_ref,
-    y_ref, state_ref, normed_ref,
+    tile, unit, groups, layout, me_ref, taps_ref, bias_ref, gain_conv_ref, gain_mlp_ref, in_ref, out_ref, pick_hbm, *refs
 ):
+    *x_refs, y_ref, pick_ref, state_ref, normed_ref, sem = refs
+    fetch = pltpu.make_async_copy(pick_hbm, pick_ref, sem)
     layer = pl.program_id(0)
     layers = pl.num_programs(0)
-    rows, channels = x_ref.shape
+    rows, channels = state_ref.shape
     pad = (normed_ref.shape[1] - rows) // 2
     now = lax.rem(layer, 2)
 
@@ -42,10 +45,22 @@
         for slot in range(2):
             normed_ref[slot, :pad] = jnp.zeros((pad, channels), jnp.bfloat16)
             normed_ref[slot, pad + rows :] = jnp.zeros((pad, channels), jnp.bfloat16)
+        for x_ref, (blocks, relative, offset) in zip(x_refs, layout):
+            width = x_ref.shape[0] // len(blocks)
+            if width == unit and not relative:
+                state_ref[...] = x_ref[...]
+                continue
+            for i, block in enumerate(blocks):
+                block = lax.bitwise_xor(me_ref[0], block) if relative else block
+                at = pl.multiple_of(block * unit + offset, ROWS)
+                state_ref[pl.ds(at, width)] = x_ref[i * width : (i + 1) * width]
         for start in range(0, rows, tile):
-            block = x_ref[start : start + tile]
-            state_ref[start : start + tile] = block
-            normed_ref[0, pad + start : pad + start + tile] = rms_scale(block.astype(jnp.float32), gain_conv_ref[0:1])
+            wide = state_ref[start : start + tile].astype(jnp.float32)
+            normed_ref[0, pad + start : pad + start + tile] = rms_scale(wide, gain_conv_ref[0:1])
+
+    @pl.when(layer == layers - 2)
+    def _():
+        fetch.start()
 
     shift = lax.shift_left(unit, layer)
     gain_next = gain_conv_ref[pl.ds(jnp.minimum(layer + 1, layers - 1), 1)]
@@ -73,6 +88,7 @@
 
     @pl.when(layer == layers - 1)
     def _():
+        fetch.wait()
         width = y_ref.shape[1] // groups
         for g in range(groups):
             part = state_ref[g * width : (g + 1) * width]
@@ -97,14 +113,16 @@
     return pick.astype(jnp.bfloat16)
 
 
-def tower(x, conv_weight, conv_bias, conv_gain, mlp_gain, w_in, w_out, unit, per, groups):
-    rows, channels = x.shape
+def tower(parts, layout, conv_weight, conv_bias, conv_gain, mlp_gain, w_in, w_out, unit, per, groups):
+    rows, channels = sum(part.shape[0] for part in parts), parts[0].shape[1]
     layers, _, hidden = w_in.shape
     pick = picker(channels, per, groups)
     out_shape = (pick.shape[1], rows // (groups + 1) * groups if groups > 1 else rows)
     pad = unit * 2 ** (layers - 1)
     tile = TILE if rows % TILE == 0 else rows
 
+    anywhere = pl.BlockSpec(memory_space=pl.ANY)
+
     def whole(shape):
         return pl.BlockSpec(shape, lambda layer: (0,) * len(shape))
 
@@ -112,33 +130,36 @@
         return pl.BlockSpec((1, *shape), lambda layer: (layer, 0, 0))
 
     return pl.pallas_call(
-        functools.partial(tower_kernel, tile, unit, groups),
+        functools.partial(tower_kernel, tile, unit, groups, layout),
         grid=(layers,),
         in_specs=[
-            whole(x.shape),
+            pl.BlockSpec(memory_space=pltpu.SMEM),
             of_layer(3 * channels, channels),
             whole(conv_bias.shape),
             whole(conv_gain.shape),
             whole(mlp_gain.shape),
             of_layer(channels, hidden),
             of_layer(hidden, channels),
-            whole(pick.shape),
+            anywhere,
+            *[whole(part.shape) for part in parts],
         ],
         out_specs=whole(out_shape),
         out_shape=jax.ShapeDtypeStruct(out_shape, jnp.bfloat16),
         scratch_shapes=[
+            pltpu.VMEM(pick.shape, jnp.bfloat16),
             pltpu.VMEM((rows, channels), jnp.bfloat16),
             pltpu.VMEM((2, rows + 2 * pad, channels), jnp.bfloat16),
+            pltpu.SemaphoreType.DMA,
         ],
         cost_estimate=pl.CostEstimate(
             flops=2 * rows * conv_weight.size + 4 * rows * w_in.size,
-            bytes_accessed=2 * (conv_weight.size + 2 * w_in.size + 2 * x.size),
+            bytes_accessed=2 * (conv_weight.size + 2 * w_in.size + 2 * rows * channels),
             transcendentals=layers * rows * (channels + hidden),
         ),
         compiler_params=pltpu.CompilerParams(vmem_limit_bytes=56 * 2**20),
         name="tower",
     )(
-        x,
+        lax.axis_index(AXIS).reshape(1).astype(jnp.int32),
         conv_weight.reshape(layers, 3 * channels, channels),
         conv_bias,
         conv_gain,
@@ -146,6 +167,7 @@
         w_in,
         w_out,
         jnp.asarray(pick),
+        *parts,
     )
 
 
@@ -228,6 +250,32 @@
     return lax.all_to_all(x, AXIS, split_axis=0, concat_axis=0, tiled=True)
 
 
+def staged(x, other):
+    me = lax.axis_index(AXIS)
+    devices = lax.axis_size(AXIS)
+    blocks, masks = [x], [0]
+    for low, bits in STAGES:
+        ways = 2**bits
+        mine = lax.bitwise_and(lax.shift_right_logical(me, low), ways - 1)
+        width = blocks[0].shape[0] // ways
+        groups = []
+        for mask in range(ways):
+            at = lax.bitwise_xor(mine, mask) * width
+            cut = [lax.dynamic_slice_in_dim(block, at, width) for block in blocks]
+            cut = cut[0] if len(cut) == 1 else jnp.concatenate(cut, axis=0)
+            if mask:
+                route = [(i, i ^ (mask << low)) for i in range(devices)]
+                if low == STAGES[0][0] and mask == TIE:
+                    ahead, other = lax.optimization_barrier((lax.ppermute(cut[:ROWS], AXIS, route), other))
+                    cut = jnp.concatenate([ahead, lax.ppermute(cut[ROWS:], AXIS, route)], axis=0)
+                else:
+                    cut = lax.ppermute(cut, AXIS, route)
+            groups.append(cut)
+        masks = [(mask << low) ^ old for mask in range(ways) for old in masks]
+        blocks = [group[at : at + width] for group in groups for at in range(0, group.shape[0], width)]
+    return groups, masks, other
+
+
 def shards(activations, conv_weight, conv_bias, conv_gain, mlp_gain, w_in, w_out):
     devices = lax.axis_size(AXIS)
     rows, channels = activations.shape
@@ -236,19 +284,32 @@
     spare = ROWS - per
     groups = per // spare if 0 < spare < per and per % spare == 0 else 1
     part = unit // CHUNKS
-    if groups > 1 and part % ROWS == 0 and part * devices % ((groups + 1) * 128) == 0 and devices * part % 128 == 0:
+    half = part // 2
+    even = half % ROWS == 0 and 128 % part == 0 and devices * part % ((groups + 1) * 128) == 0
+    if groups > 1 and even and devices == 2 ** sum(bits for _, bits in STAGES):
         size = rows // CHUNKS
-        y = None
+        every = tuple(range(devices))
         towers = []
         for c in range(CHUNKS):
-            whole = activations if c == 0 else lax.optimization_barrier(activations)
-            x = exchange(whole[c * size : (c + 1) * size])
-            towers.append(tower(x, *weights, part, per, groups))
+            if c == 0:
+                x = activations[:size].reshape(devices, 2, half, channels)
+                parts, masks, whole = staged(x[:, 1].reshape(-1, channels), x[:, 0])
+                parts = [exchange(whole), *parts]
+                layout = [(every, False, 0)]
+                held = devices // (len(parts) - 1)
+                for i in range(len(parts) - 1):
+                    layout.append((tuple(masks[i * held : (i + 1) * held]), True, half))
+            else:
+                x = lax.optimization_barrier(activations)[c * size : (c + 1) * size]
+                parts, layout = [exchange(x)], [(every, False, 0)]
+            parts = [x.reshape(-1, channels) for x in parts]
+            towers.append(tower(parts, tuple(layout), *weights, part, per, groups))
+        y = None
         for c in range(CHUNKS):
             x = exchange(towers[c].reshape(devices, ROWS, -1))
             y = weave(x, y, per, groups, part, c * size, rows)
         return y
-    y = tower(exchange(activations), *weights, unit, per, 1)
+    y = tower([exchange(activations)], ((tuple(range(devices)), False, 0),), *weights, unit, per, 1)
     y = exchange(y.reshape(devices, per, rows))
     y = y.reshape(devices, per, devices, unit).transpose(1, 2, 0, 3)
     return y.reshape(per, devices * rows)

time: 105 us -> 104 us (level)
  waiting for transfers between devices: 43.5 us -> 33.4 us
  starting transfers between devices: 18.2 us -> 27.7 us
  Pallas kernels: 39.5 us -> 37.9 us
  local copies, waits for them, and re-layouts: 3.2 us -> 4.32 us
    all_to_all x4, waiting for transfers between devices: 43.5 us -> 24.5 us  [exchange(): return lax.all_to_all(x, AXIS, split_axis=0, concat_axis=0, tiled=True)]
    ppermute x0 -> x8, starting transfers between devices: none -> 11.3 us  [the longest x6 8.06 us: staged(): cut = lax.ppermute(cut, AXIS, route)]
    ppermute x0 -> x8, waiting for transfers between devices: none -> 8.97 us  [the longest x6 8.96 us: staged(): cut = lax.ppermute(cut, AXIS, route)]
    all_to_all x4, starting transfers between devices: 18.2 us -> 16.4 us  [exchange(): return lax.all_to_all(x, AXIS, split_axis=0, concat_axis=0, tiled=True)]
    pallas_call x2, Pallas kernels: 36.3 us -> 34.7 us  [tower(): pl.pallas_call(functools.partial(tower_kernel, tile, unit, groups, layout...]
    slice x2 -> x6, local copies, waits for them, and re-layouts: 3.18 us -> 2.33 us  [the longest x1 1.33 us: shards(): x = activations[:size].reshape(devices, 2, half, channels)]
  transfers between devices with their start and end apart: 4 -> 12, of which waited for: 4 -> 9; matrix products, arithmetic and copies ran while one was open for 1% -> 1% of each run, Pallas kernels for 36% -> 35%
where the time goes in v4:
time: 104 us
  Pallas kernels  37.9 us (36%)
  waiting for transfers between devices  33.4 us (32%)
  starting transfers between devices  27.7 us (27%)
  local copies, waits for them, and re-layouts  4.32 us (4%)
    pallas_call x2, Pallas kernels, tower(): pl.pallas_call(functools.partial(tower_kernel, tile, unit, groups, layout...  34.7 us
    all_to_all x4, waiting for transfers between devices, exchange(): return lax.all_to_all(x, AXIS, split_axis=0, concat_axis=0, tiled=True)  24.5 us
    all_to_all x4, starting transfers between devices, exchange(): return lax.all_to_all(x, AXIS, split_axis=0, concat_axis=0, tiled=True)  16.4 us
    ppermute x6, waiting for transfers between devices, staged(): cut = lax.ppermute(cut, AXIS, route)  8.96 us
    ppermute x6, starting transfers between devices, staged(): cut = lax.ppermute(cut, AXIS, route)  8.06 us
    pallas_call x2, Pallas kernels, weave(): pl.pallas_call(functools.partial(weave_kernel, per, groups, unit, first,...  3.2 us
    ppermute x1, starting transfers between devices, staged(): lax.ppermute(cut[ROWS:], AXIS, route)  3.09 us
  transfers between devices with their start and end apart: 12, of which 9 were waited for; matrix products, arithmetic and copies ran while one was open for 1% of the time, Pallas kernels for 35%

profile of v4, /device:TPU:0, one launch (start us, length us, event | category | flops | bytes accessed | tf_op | source)
XLA Modules:
  0.0 103.6 jit_solution(17317872967440793568)
XLA Ops:
  0.0 1.3 %slice.55 = bf16[1024,384]{1,0:T(8,128)(2,1)S(1)} slice(bf16[2048,384]{1,0:T(8,128)(2,1)} %param.11), slice={[0:1024], [0:384]} | slice | bytes 1572864 | tf_op jit(solution)/shard_map/slice | solution.py:295
  1.3 0.8 slice_bitcast_fusion
  2.2 3.1 %collective-permute-start.1 = (bf16[112,384]{1,0:T(8,128)(2,1)S(1)}, bf16[112,384]{1,0:T(8,128)(2,1)S(1)}, u32[]{:S(2)}, u32[]{:S(2)}) collective-permute-start(bf16[112,384]{1,0:T(8,128)(2,1)S(1)} %constant_dynamic-slice_fusion.15), channel_id=1, source_target_pairs={{0,8},{1,9},{2,10},{3,11},{4,12},{5,13},{6,14},{7,15},{8,0},{9,1},... | collective-permute-start | bytes 258056 | tf_op jit(solution)/shard_map/ppermute | solution.py:270
  5.4 4.1 %collective-permute-start.3 = (bf16[128,384]{1,0:T(8,128)(2,1)S(1)}, bf16[128,384]{1,0:T(8,128)(2,1)S(1)}, u32[]{:S(2)}, u32[]{:S(2)}) collective-permute-start(bf16[128,384]{1,0:T(8,128)(2,1)S(1)} %get-tuple-element.17), channel_id=1, source_target_pairs={{0,24},{1,25},{2,26},{3,27},{4,28},{5,29},{6,30},{7,31},{8,16},{9,... | collective-permute-start | bytes 294920 | tf_op jit(solution)/shard_map/ppermute | solution.py:272
  9.6 1.0 slice.72
  10.5 5.2 %all-to-all-start.2 = ((bf16[32,16,384]{2,1,0:T(8,128)(2,1)}), bf16[32,16,384]{2,1,0:T(8,128)(2,1)S(1)}, u32[]{:S(2)}, u32[]{:S(2)}) async-start(bf16[32,16,384]{2,1,0:T(8,128)(2,1)} %get-tuple-element.7), calls=%async_computation.2 | async-start | bytes 786432 | tf_op jit(solution)/shard_map/all_to_all | solution.py:250
  15.8 1.7 %collective-permute-done.2 = bf16[128,384]{1,0:T(8,128)(2,1)S(1)} collective-permute-done((bf16[128,384]{1,0:T(8,128)(2,1)S(1)}, bf16[128,384]{1,0:T(8,128)(2,1)S(1)}, u32[]{:S(2)}, u32[]{:S(2)}) %collective-permute-start.2) | collective-permute-done | bytes 98336 | tf_op jit(solution)/shard_map/ppermute | solution.py:272
  17.5 1.6 %collective-permute-start.4 = (bf16[128,384]{1,0:T(8,128)(2,1)S(1)}, bf16[128,384]{1,0:T(8,128)(2,1)S(1)}, u32[]{:S(2)}, u32[]{:S(2)}) collective-permute-start(bf16[128,384]{1,0:T(8,128)(2,1)S(1)} %pad_maximum_fusion), channel_id=1, source_target_pairs={{0,2},{1,3},{2,0},{3,1},{4,6},{5,7},{6,4},{7,5},{8,10},{9,11},{10,... | collective-permute-start | bytes 294920 | tf_op jit(solution)/shard_map/ppermute | solution.py:272
  19.1 1.6 %collective-permute-start.5 = (bf16[128,384]{1,0:T(8,128)(2,1)S(1)}, bf16[128,384]{1,0:T(8,128)(2,1)S(1)}, u32[]{:S(2)}, u32[]{:S(2)}) collective-permute-start(bf16[128,384]{1,0:T(8,128)(2,1)S(1)} %pad_maximum_fusion.1), channel_id=1, source_target_pairs={{0,4},{1,5},{2,6},{3,7},{4,0},{5,1},{6,2},{7,3},{8,12},{9,13},{10,... | collective-permute-start | bytes 294920 | tf_op jit(solution)/shard_map/ppermute | solution.py:272
  21.3 3.4 %collective-permute-done.4 = bf16[128,384]{1,0:T(8,128)(2,1)S(1)} collective-permute-done((bf16[128,384]{1,0:T(8,128)(2,1)S(1)}, bf16[128,384]{1,0:T(8,128)(2,1)S(1)}, u32[]{:S(2)}, u32[]{:S(2)}) %collective-permute-start.4) | collective-permute-done | bytes 98336 | tf_op jit(solution)/shard_map/ppermute | solution.py:272
  24.8 1.3 %collective-permute-done.5 = bf16[128,384]{1,0:T(8,128)(2,1)S(1)} collective-permute-done((bf16[128,384]{1,0:T(8,128)(2,1)S(1)}, bf16[128,384]{1,0:T(8,128)(2,1)S(1)}, u32[]{:S(2)}, u32[]{:S(2)}) %collective-permute-start.5) | collective-permute-done | bytes 98336 | tf_op jit(solution)/shard_map/ppermute | solution.py:272
  26.2 1.4 %collective-permute-done.6 = bf16[128,384]{1,0:T(8,128)(2,1)S(1)} collective-permute-done((bf16[128,384]{1,0:T(8,128)(2,1)S(1)}, bf16[128,384]{1,0:T(8,128)(2,1)S(1)}, u32[]{:S(2)}, u32[]{:S(2)}) %collective-permute-start.6) | collective-permute-done | bytes 98336 | tf_op jit(solution)/shard_map/ppermute | solution.py:272
  27.6 1.3 %all-to-all-done.2 = bf16[32,16,384]{2,1,0:T(8,128)(2,1)S(1)} async-done(((bf16[32,16,384]{2,1,0:T(8,128)(2,1)}), bf16[32,16,384]{2,1,0:T(8,128)(2,1)S(1)}, u32[]{:S(2)}, u32[]{:S(2)}) %all-to-all-start.2) | async-done | bytes 393248 | tf_op jit(solution)/shard_map/all_to_all | solution.py:250
  28.9 2.7 %all-to-all-start = ((bf16[32,32,384]{2,1,0:T(8,128)(2,1)}), bf16[32,32,384]{2,1,0:T(8,128)(2,1)S(1)}, u32[]{:S(2)}, u32[]{:S(2)}) async-start(bf16[32,32,384]{2,1,0:T(8,128)(2,1)} %bitcast.2), calls=%async_computation | async-start | bytes 1572864 | tf_op jit(solution)/shard_map/all_to_all | solution.py:250
  32.1 1.2 %collective-permute-done.7.refs_2_ = bf16[256,384]{1,0:T(8,128)(2,1)S(1)} collective-permute-done((bf16[256,384]{1,0:T(8,128)(2,1)S(1)}, bf16[256,384]{1,0:T(8,128)(2,1)S(1)}, u32[]{:S(2)}, u32[]{:S(2)}) %collective-permute-start.7) | collective-permute-done | bytes 196640 | tf_op jit(solution)/shard_map/ppermute | solution.py:272
  33.9 17.3 %tower.3 = bf16[512,768]{1,0:T(8,128)(2,1)} custom-call(s32[1]{0:T(128)} %bitcast.me_ref, bf16[4,1152,384]{2,1,0:T(8,128)(2,1)} %bitcast.24, f32[4,384]{1,0:T(4,128)} %bias_ref.3, f32[4,384]{1,0:T(4,128)} %gain_conv_ref.3, f32[4,384]{1,0:T(4,128)} %gain_mlp_ref.3, bf16[4,384,768]{2,1,0:T(8,128)(2,1)} %in_ref.3, bf16[4,768,384]{2,1,0:T(8,128)(2,1)} %out_ref.3, ...), custom_call_target="tpu_custom_call" | custom-call | flops 8455716864 | bytes 9830400 | tf_op jit(solution)/shard_map/tower/pallas_call | solution.py:132
  51.3 1.0 all-to-all-done
  52.2 4.9 %all-to-all-start.3 = ((bf16[32,16,768]{2,1,0:T(8,128)(2,1)}), bf16[32,16,768]{2,1,0:T(8,128)(2,1)S(1)}, u32[]{:S(2)}, u32[]{:S(2)}) async-start(bf16[32,16,768]{2,1,0:T(8,128)(2,1)} %bitcast.21), calls=%async_computation.3 | async-start | bytes 1572864 | tf_op jit(solution)/shard_map/all_to_all | solution.py:250
  57.2 17.4 %tower.2 = bf16[512,768]{1,0:T(8,128)(2,1)} custom-call(s32[1]{0:T(128)} %bitcast.me_ref, bf16[4,1152,384]{2,1,0:T(8,128)(2,1)} %bitcast.25, f32[4,384]{1,0:T(4,128)} %bias_ref.3, f32[4,384]{1,0:T(4,128)} %gain_conv_ref.3, f32[4,384]{1,0:T(4,128)} %gain_mlp_ref.3, bf16[4,384,768]{2,1,0:T(8,128)(2,1)} %in_ref.3, bf16[4,768,384]{2,1,0:T(8,128)(2,1)} %out_ref.3, ...), custom_call_target="tpu_custom_call" | custom-call | flops 8455716864 | bytes 9830400 | tf_op jit(solution)/shard_map/tower/pallas_call | solution.py:132
  74.5 3.2 %all-to-all-done.3.x_ref = bf16[32,16,768]{2,1,0:T(8,128)(2,1)S(1)} async-done(((bf16[32,16,768]{2,1,0:T(8,128)(2,1)}), bf16[32,16,768]{2,1,0:T(8,128)(2,1)S(1)}, u32[]{:S(2)}, u32[]{:S(2)}) %all-to-all-start.3) | async-done | bytes 786464 | tf_op jit(solution)/shard_map/all_to_all | solution.py:250
  77.8 3.6 %all-to-all-start.1 = ((bf16[32,16,768]{2,1,0:T(8,128)(2,1)}), bf16[32,16,768]{2,1,0:T(8,128)(2,1)S(1)}, u32[]{:S(2)}, u32[]{:S(2)}) async-start(bf16[32,16,768]{2,1,0:T(8,128)(2,1)} %bitcast.22), calls=%async_computation.1 | async-start | bytes 1572864 | tf_op jit(solution)/shard_map/all_to_all | solution.py:250
  81.4 1.6 %weave.2.refs_0_ = bf16[12,65536]{1,0:T(8,128)(2,1)} custom-call(bf16[32,16,768]{2,1,0:T(8,128)(2,1)S(1)} %all-to-all-done.3.x_ref, bf16[512,512]{1,0:T(8,128)(2,1)S(1)} %copy-done), custom_call_target="tpu_custom_call" | custom-call | tf_op jit(solution)/shard_map/weave/pallas_call | solution.py:234
  83.0 19.0 %all-to-all-done.1.x_ref = bf16[32,16,768]{2,1,0:T(8,128)(2,1)S(1)} async-done(((bf16[32,16,768]{2,1,0:T(8,128)(2,1)}), bf16[32,16,768]{2,1,0:T(8,128)(2,1)S(1)}, u32[]{:S(2)}, u32[]{:S(2)}) %all-to-all-start.1) | async-done | bytes 786464 | tf_op jit(solution)/shard_map/all_to_all | solution.py:250
  102.0 1.6 %weave.3 = bf16[12,65536]{1,0:T(8,128)(2,1)} custom-call(bf16[32,16,768]{2,1,0:T(8,128)(2,1)S(1)} %all-to-all-done.1.x_ref, bf16[512,512]{1,0:T(8,128)(2,1)S(1)} %copy-done, bf16[12,65536]{1,0:T(8,128)(2,1)} %weave.2.refs_0_), custom_call_target="tpu_custom_call", output_to_operand_aliasing={{}: (2, {})} | custom-call | tf_op jit(solution)/shard_map/weave/pallas_call | solution.py:234
  (49 shorter events, 2.2 us)
Async XLA Ops:
  0.0 9.5 %copy-start.1 = (bf16[2048,384]{1,0:T(8,128)(2,1)S(1)}, bf16[2048,384]{1,0:T(8,128)(2,1)}, u32[]{:S(2)}) copy-start(bf16[2048,384]{1,0:T(8,128)(2,1)} %param.11) | copy-start | bytes 4718596
  2.2 13.5 %collective-permute-start.1 = (bf16[112,384]{1,0:T(8,128)(2,1)S(1)}, bf16[112,384]{1,0:T(8,128)(2,1)S(1)}, u32[]{:S(2)}, u32[]{:S(2)}) collective-permute-start(bf16[112,384]{1,0:T(8,128)(2,1)S(1)} %constant_dynamic-slice_fusion.15), channel_id=1, source_target_pairs={{0,8},{1,9},{2,10},{3,11},{4,12},{5,13},{6,14},{7,15},{8,0},{9,1},... | collective-permute-start | bytes 258056 | tf_op jit(solution)/shard_map/ppermute | solution.py:270
  5.3 5.2 %collective-permute-start = (bf16[16,384]{1,0:T(8,128)(2,1)S(1)}, bf16[16,384]{1,0:T(8,128)(2,1)S(1)}, u32[]{:S(2)}, u32[]{:S(2)}) collective-permute-start(bf16[16,384]{1,0:T(8,128)(2,1)S(1)} %get-tuple-element.12), channel_id=1, source_target_pairs={{0,8},{1,9},{2,10},{3,11},{4,12},{5,13},{6,14},{7,15},{8,0},{9,1},... | collective-permute-start | bytes 36872 | tf_op jit(solution)/shard_map/ppermute | solution.py:269
  5.4 10.4 %collective-permute-start.3 = (bf16[128,384]{1,0:T(8,128)(2,1)S(1)}, bf16[128,384]{1,0:T(8,128)(2,1)S(1)}, u32[]{:S(2)}, u32[]{:S(2)}) collective-permute-start(bf16[128,384]{1,0:T(8,128)(2,1)S(1)} %get-tuple-element.17), channel_id=1, source_target_pairs={{0,24},{1,25},{2,26},{3,27},{4,28},{5,29},{6,30},{7,31},{8,16},{9,... | collective-permute-start | bytes 294920 | tf_op jit(solution)/shard_map/ppermute | solution.py:272
  9.5 8.0 %collective-permute-start.2 = (bf16[128,384]{1,0:T(8,128)(2,1)S(1)}, bf16[128,384]{1,0:T(8,128)(2,1)S(1)}, u32[]{:S(2)}, u32[]{:S(2)}) collective-permute-start(bf16[128,384]{1,0:T(8,128)(2,1)S(1)} %get-tuple-element.18), channel_id=1, source_target_pairs={{0,16},{1,17},{2,18},{3,19},{4,20},{5,21},{6,22},{7,23},{8,24},{9,... | collective-permute-start | bytes 294920 | tf_op jit(solution)/shard_map/ppermute | solution.py:272
  10.5 18.4 %all-to-all-start.2 = ((bf16[32,16,384]{2,1,0:T(8,128)(2,1)}), bf16[32,16,384]{2,1,0:T(8,128)(2,1)S(1)}, u32[]{:S(2)}, u32[]{:S(2)}) async-start(bf16[32,16,384]{2,1,0:T(8,128)(2,1)} %get-tuple-element.7), calls=%async_computation.2 | async-start | bytes 786432 | tf_op jit(solution)/shard_map/all_to_all | solution.py:250
  17.5 7.2 %collective-permute-start.4 = (bf16[128,384]{1,0:T(8,128)(2,1)S(1)}, bf16[128,384]{1,0:T(8,128)(2,1)S(1)}, u32[]{:S(2)}, u32[]{:S(2)}) collective-permute-start(bf16[128,384]{1,0:T(8,128)(2,1)S(1)} %pad_maximum_fusion), channel_id=1, source_target_pairs={{0,2},{1,3},{2,0},{3,1},{4,6},{5,7},{6,4},{7,5},{8,10},{9,11},{10,... | collective-permute-start | bytes 294920 | tf_op jit(solution)/shard_map/ppermute | solution.py:272
  19.1 7.0 %collective-permute-start.5 = (bf16[128,384]{1,0:T(8,128)(2,1)S(1)}, bf16[128,384]{1,0:T(8,128)(2,1)S(1)}, u32[]{:S(2)}, u32[]{:S(2)}) collective-permute-start(bf16[128,384]{1,0:T(8,128)(2,1)S(1)} %pad_maximum_fusion.1), channel_id=1, source_target_pairs={{0,4},{1,5},{2,6},{3,7},{4,0},{5,1},{6,2},{7,3},{8,12},{9,13},{10,... | collective-permute-start | bytes 294920 | tf_op jit(solution)/shard_map/ppermute | solution.py:272
  20.7 6.9 %collective-permute-start.6 = (bf16[128,384]{1,0:T(8,128)(2,1)S(1)}, bf16[128,384]{1,0:T(8,128)(2,1)S(1)}, u32[]{:S(2)}, u32[]{:S(2)}) collective-permute-start(bf16[128,384]{1,0:T(8,128)(2,1)S(1)} %pad_maximum_fusion.2), channel_id=1, source_target_pairs={{0,6},{1,7},{2,4},{3,5},{4,2},{5,3},{6,0},{7,1},{8,14},{9,15},{10,... | collective-permute-start | bytes 294920 | tf_op jit(solution)/shard_map/ppermute | solution.py:272
  28.9 4.4 %copy-start.3 = (bf16[32,16,384]{2,1,0:T(8,128)(2,1)}, bf16[32,16,384]{2,1,0:T(8,128)(2,1)S(1)}, u32[]{:S(2)}) copy-start(bf16[32,16,384]{2,1,0:T(8,128)(2,1)S(1)} %all-to-all-done.2) | copy-start | bytes 1179652
  28.9 23.4 %all-to-all-start = ((bf16[32,32,384]{2,1,0:T(8,128)(2,1)}), bf16[32,32,384]{2,1,0:T(8,128)(2,1)S(1)}, u32[]{:S(2)}, u32[]{:S(2)}) async-start(bf16[32,32,384]{2,1,0:T(8,128)(2,1)} %bitcast.2), calls=%async_computation | async-start | bytes 1572864 | tf_op jit(solution)/shard_map/all_to_all | solution.py:250
  31.7 1.5 %copy-start.4 = (bf16[256,384]{1,0:T(8,128)(2,1)}, bf16[256,384]{1,0:T(8,128)(2,1)S(1)}, u32[]{:S(2)}) copy-start(bf16[256,384]{1,0:T(8,128)(2,1)S(1)} %get-tuple-element.47.refs_1_) | copy-start | bytes 589828
  31.8 1.5 %collective-permute-start.7 = (bf16[256,384]{1,0:T(8,128)(2,1)S(1)}, bf16[256,384]{1,0:T(8,128)(2,1)S(1)}, u32[]{:S(2)}, u32[]{:S(2)}) collective-permute-start(bf16[256,384]{1,0:T(8,128)(2,1)S(1)} %get-tuple-element.46), channel_id=1, source_target_pairs={{0,1},{1,0},{2,3},{3,2},{4,5},{5,4},{6,7},{7,6},{8,9},{9,8},{10,11... | collective-permute-start | bytes 589832 | tf_op jit(solution)/shard_map/ppermute | solution.py:272
  33.3 0.7 copy-start.5
  52.2 4.9 %copy-start.2 = (bf16[32,32,384]{2,1,0:T(8,128)(2,1)}, bf16[32,32,384]{2,1,0:T(8,128)(2,1)S(1)}, u32[]{:S(2)}) copy-start(bf16[32,32,384]{2,1,0:T(8,128)(2,1)S(1)} %all-to-all-done) | copy-start | bytes 2359300
  52.2 25.5 %all-to-all-start.3 = ((bf16[32,16,768]{2,1,0:T(8,128)(2,1)}), bf16[32,16,768]{2,1,0:T(8,128)(2,1)S(1)}, u32[]{:S(2)}, u32[]{:S(2)}) async-start(bf16[32,16,768]{2,1,0:T(8,128)(2,1)} %bitcast.21), calls=%async_computation.3 | async-start | bytes 1572864 | tf_op jit(solution)/shard_map/all_to_all | solution.py:250
  57.1 24.2 %copy-start = (bf16[512,512]{1,0:T(8,128)(2,1)S(1)}, bf16[512,512]{1,0:T(8,128)(2,1)}, u32[]{:S(2)}) copy-start(bf16[512,512]{1,0:T(8,128)(2,1)} %constant.135.clone.weave_ref) | copy-start | bytes 1572868
  77.8 24.2 %all-to-all-start.1 = ((bf16[32,16,768]{2,1,0:T(8,128)(2,1)}), bf16[32,16,768]{2,1,0:T(8,128)(2,1)S(1)}, u32[]{:S(2)}, u32[]{:S(2)}) async-start(bf16[32,16,768]{2,1,0:T(8,128)(2,1)} %bitcast.22), calls=%async_computation.1 | async-start | bytes 1572864 | tf_op jit(solution)/shard_map/all_to_all | solution.py:250

commit v5 on v4

--- a/solution.py
+++ b/solution.py
@@ -294,6 +294,7 @@
             if c == 0:
                 x = activations[:size].reshape(devices, 2, half, channels)
                 parts, masks, whole = staged(x[:, 1].reshape(-1, channels), x[:, 0])
+                settled = parts[-1]
                 parts = [exchange(whole), *parts]
                 layout = [(every, False, 0)]
                 held = devices // (len(parts) - 1)
@@ -301,6 +302,7 @@
                     layout.append((tuple(masks[i * held : (i + 1) * held]), True, half))
             else:
                 x = lax.optimization_barrier(activations)[c * size : (c + 1) * size]
+                x, _ = lax.optimization_barrier((x, settled))
                 parts, layout = [exchange(x)], [(every, False, 0)]
             parts = [x.reshape(-1, channels) for x in parts]
             towers.append(tower(parts, tuple(layout), *weights, part, per, groups))

time: 104 us -> 103 us (level)
  transfers between devices with their start and end apart: 12 -> 12, of which waited for: 9 -> 8; matrix products, arithmetic and copies ran while one was open for 1% -> 1% of each run, Pallas kernels for 35% -> 35%
where the time goes in v5:
time: 103 us
  Pallas kernels  37.9 us (37%)
  waiting for transfers between devices  34.3 us (33%)
  starting transfers between devices  26.9 us (26%)
  local copies, waits for them, and re-layouts  3.53 us (3%)
    pallas_call x2, Pallas kernels, tower(): pl.pallas_call(functools.partial(tower_kernel, tile, unit, groups, layout...  34.7 us
    all_to_all x4, waiting for transfers between devices, exchange(): return lax.all_to_all(x, AXIS, split_axis=0, concat_axis=0, tiled=True)  25.5 us
    all_to_all x4, starting transfers between devices, exchange(): return lax.all_to_all(x, AXIS, split_axis=0, concat_axis=0, tiled=True)  15.9 us
    ppermute x6, waiting for transfers between devices, staged(): cut = lax.ppermute(cut, AXIS, route)  8.78 us
    ppermute x6, starting transfers between devices, staged(): cut = lax.ppermute(cut, AXIS, route)  7.81 us
    pallas_call x2, Pallas kernels, weave(): pl.pallas_call(functools.partial(weave_kernel, per, groups, unit, first,...  3.21 us
    ppermute x1, starting transfers between devices, staged(): lax.ppermute(cut[ROWS:], AXIS, route)  3.09 us
  transfers between devices with their start and end apart: 12, of which 8 were waited for; matrix products, arithmetic and copies ran while one was open for 1% of the time, Pallas kernels for 35%

profile of v5, /device:TPU:0, one launch (start us, length us, event | category | flops | bytes accessed | tf_op | source)
XLA Modules:
  0.0 102.9 jit_solution(12700485720800937575)
XLA Ops:
  0.0 1.2 %slice.55 = bf16[1024,384]{1,0:T(8,128)(2,1)S(1)} slice(bf16[2048,384]{1,0:T(8,128)(2,1)} %param.11), slice={[0:1024], [0:384]} | slice | bytes 1572864 | tf_op jit(solution)/shard_map/slice | solution.py:295
  1.2 0.8 slice_bitcast_fusion
  2.1 3.1 %collective-permute-start.1 = (bf16[112,384]{1,0:T(8,128)(2,1)S(1)}, bf16[112,384]{1,0:T(8,128)(2,1)S(1)}, u32[]{:S(2)}, u32[]{:S(2)}) collective-permute-start(bf16[112,384]{1,0:T(8,128)(2,1)S(1)} %constant_dynamic-slice_fusion.15), channel_id=1, source_target_pairs={{0,8},{1,9},{2,10},{3,11},{4,12},{5,13},{6,14},{7,15},{8,0},{9,1},... | collective-permute-start | bytes 258056 | tf_op jit(solution)/shard_map/ppermute | solution.py:270
  5.3 4.1 %collective-permute-start.3 = (bf16[128,384]{1,0:T(8,128)(2,1)S(1)}, bf16[128,384]{1,0:T(8,128)(2,1)S(1)}, u32[]{:S(2)}, u32[]{:S(2)}) collective-permute-start(bf16[128,384]{1,0:T(8,128)(2,1)S(1)} %get-tuple-element.19), channel_id=1, source_target_pairs={{0,24},{1,25},{2,26},{3,27},{4,28},{5,29},{6,30},{7,31},{8,16},{9,... | collective-permute-start | bytes 294920 | tf_op jit(solution)/shard_map/ppermute | solution.py:272
  9.4 5.2 %all-to-all-start.2 = ((bf16[32,16,384]{2,1,0:T(8,128)(2,1)}), bf16[32,16,384]{2,1,0:T(8,128)(2,1)S(1)}, u32[]{:S(2)}, u32[]{:S(2)}) async-start(bf16[32,16,384]{2,1,0:T(8,128)(2,1)} %get-tuple-element.10), calls=%async_computation.2 | async-start | bytes 786432 | tf_op jit(solution)/shard_map/all_to_all | solution.py:250
  14.8 2.6 %collective-permute-done.2 = bf16[128,384]{1,0:T(8,128)(2,1)S(1)} collective-permute-done((bf16[128,384]{1,0:T(8,128)(2,1)S(1)}, bf16[128,384]{1,0:T(8,128)(2,1)S(1)}, u32[]{:S(2)}, u32[]{:S(2)}) %collective-permute-start.2) | collective-permute-done | bytes 98336 | tf_op jit(solution)/shard_map/ppermute | solution.py:272
  17.4 1.6 %collective-permute-start.4 = (bf16[128,384]{1,0:T(8,128)(2,1)S(1)}, bf16[128,384]{1,0:T(8,128)(2,1)S(1)}, u32[]{:S(2)}, u32[]{:S(2)}) collective-permute-start(bf16[128,384]{1,0:T(8,128)(2,1)S(1)} %pad_maximum_fusion), channel_id=1, source_target_pairs={{0,2},{1,3},{2,0},{3,1},{4,6},{5,7},{6,4},{7,5},{8,10},{9,11},{10,... | collective-permute-start | bytes 294920 | tf_op jit(solution)/shard_map/ppermute | solution.py:272
  19.0 1.6 %collective-permute-start.5 = (bf16[128,384]{1,0:T(8,128)(2,1)S(1)}, bf16[128,384]{1,0:T(8,128)(2,1)S(1)}, u32[]{:S(2)}, u32[]{:S(2)}) collective-permute-start(bf16[128,384]{1,0:T(8,128)(2,1)S(1)} %pad_maximum_fusion.1), channel_id=1, source_target_pairs={{0,4},{1,5},{2,6},{3,7},{4,0},{5,1},{6,2},{7,3},{8,12},{9,13},{10,... | collective-permute-start | bytes 294920 | tf_op jit(solution)/shard_map/ppermute | solution.py:272
  20.6 0.5 collective-permute-start.6
  21.2 3.0 %collective-permute-done.4 = bf16[128,384]{1,0:T(8,128)(2,1)S(1)} collective-permute-done((bf16[128,384]{1,0:T(8,128)(2,1)S(1)}, bf16[128,384]{1,0:T(8,128)(2,1)S(1)}, u32[]{:S(2)}, u32[]{:S(2)}) %collective-permute-start.4) | collective-permute-done | bytes 98336 | tf_op jit(solution)/shard_map/ppermute | solution.py:272
  24.3 1.0 collective-permute-done.5
  25.4 1.7 %collective-permute-done.6 = bf16[128,384]{1,0:T(8,128)(2,1)S(1)} collective-permute-done((bf16[128,384]{1,0:T(8,128)(2,1)S(1)}, bf16[128,384]{1,0:T(8,128)(2,1)S(1)}, u32[]{:S(2)}, u32[]{:S(2)}) %collective-permute-start.6) | collective-permute-done | bytes 98336 | tf_op jit(solution)/shard_map/ppermute | solution.py:272
  27.3 1.0 slice.72
  28.3 0.5 collective-permute-done.7.refs_2_
  28.7 3.4 %all-to-all-start = ((bf16[32,32,384]{2,1,0:T(8,128)(2,1)}), bf16[32,32,384]{2,1,0:T(8,128)(2,1)S(1)}, u32[]{:S(2)}, u32[]{:S(2)}) async-start(bf16[32,32,384]{2,1,0:T(8,128)(2,1)} %bitcast.5), calls=%async_computation | async-start | bytes 1572864 | tf_op jit(solution)/shard_map/all_to_all | solution.py:250
  32.2 17.3 %tower.3 = bf16[512,768]{1,0:T(8,128)(2,1)} custom-call(s32[1]{0:T(128)} %bitcast.me_ref, bf16[4,1152,384]{2,1,0:T(8,128)(2,1)} %bitcast.24, f32[4,384]{1,0:T(4,128)} %bias_ref.3, f32[4,384]{1,0:T(4,128)} %gain_conv_ref.3, f32[4,384]{1,0:T(4,128)} %gain_mlp_ref.3, bf16[4,384,768]{2,1,0:T(8,128)(2,1)} %in_ref.3, bf16[4,768,384]{2,1,0:T(8,128)(2,1)} %out_ref.3, ...), custom_call_target="tpu_custom_call" | custom-call | flops 8455716864 | bytes 9830400 | tf_op jit(solution)/shard_map/tower/pallas_call | solution.py:132
  49.6 3.3 %all-to-all-done = bf16[32,32,384]{2,1,0:T(8,128)(2,1)S(1)} async-done(((bf16[32,32,384]{2,1,0:T(8,128)(2,1)}), bf16[32,32,384]{2,1,0:T(8,128)(2,1)S(1)}, u32[]{:S(2)}, u32[]{:S(2)}) %all-to-all-start) | async-done | bytes 786464 | tf_op jit(solution)/shard_map/all_to_all | solution.py:250
  52.8 3.6 %all-to-all-start.3 = ((bf16[32,16,768]{2,1,0:T(8,128)(2,1)}), bf16[32,16,768]{2,1,0:T(8,128)(2,1)S(1)}, u32[]{:S(2)}, u32[]{:S(2)}) async-start(bf16[32,16,768]{2,1,0:T(8,128)(2,1)} %bitcast.21), calls=%async_computation.3 | async-start | bytes 1572864 | tf_op jit(solution)/shard_map/all_to_all | solution.py:250
  56.5 17.3 %tower.2 = bf16[512,768]{1,0:T(8,128)(2,1)} custom-call(s32[1]{0:T(128)} %bitcast.me_ref, bf16[4,1152,384]{2,1,0:T(8,128)(2,1)} %bitcast.25, f32[4,384]{1,0:T(4,128)} %bias_ref.3, f32[4,384]{1,0:T(4,128)} %gain_conv_ref.3, f32[4,384]{1,0:T(4,128)} %gain_mlp_ref.3, bf16[4,384,768]{2,1,0:T(8,128)(2,1)} %in_ref.3, bf16[4,768,384]{2,1,0:T(8,128)(2,1)} %out_ref.3, ...), custom_call_target="tpu_custom_call" | custom-call | flops 8455716864 | bytes 9830400 | tf_op jit(solution)/shard_map/tower/pallas_call | solution.py:132
  73.8 3.2 %all-to-all-done.3.x_ref = bf16[32,16,768]{2,1,0:T(8,128)(2,1)S(1)} async-done(((bf16[32,16,768]{2,1,0:T(8,128)(2,1)}), bf16[32,16,768]{2,1,0:T(8,128)(2,1)S(1)}, u32[]{:S(2)}, u32[]{:S(2)}) %all-to-all-start.3) | async-done | bytes 786464 | tf_op jit(solution)/shard_map/all_to_all | solution.py:250
  77.1 3.6 %all-to-all-start.1 = ((bf16[32,16,768]{2,1,0:T(8,128)(2,1)}), bf16[32,16,768]{2,1,0:T(8,128)(2,1)S(1)}, u32[]{:S(2)}, u32[]{:S(2)}) async-start(bf16[32,16,768]{2,1,0:T(8,128)(2,1)} %bitcast.22), calls=%async_computation.1 | async-start | bytes 1572864 | tf_op jit(solution)/shard_map/all_to_all | solution.py:250
  80.7 1.6 %weave.2.refs_0_ = bf16[12,65536]{1,0:T(8,128)(2,1)} custom-call(bf16[32,16,768]{2,1,0:T(8,128)(2,1)S(1)} %all-to-all-done.3.x_ref, bf16[512,512]{1,0:T(8,128)(2,1)S(1)} %copy-done), custom_call_target="tpu_custom_call" | custom-call | tf_op jit(solution)/shard_map/weave/pallas_call | solution.py:234
  82.3 19.0 %all-to-all-done.1.x_ref = bf16[32,16,768]{2,1,0:T(8,128)(2,1)S(1)} async-done(((bf16[32,16,768]{2,1,0:T(8,128)(2,1)}), bf16[32,16,768]{2,1,0:T(8,128)(2,1)S(1)}, u32[]{:S(2)}, u32[]{:S(2)}) %all-to-all-start.1) | async-done | bytes 786464 | tf_op jit(solution)/shard_map/all_to_all | solution.py:250
  101.3 1.6 %weave.3 = bf16[12,65536]{1,0:T(8,128)(2,1)} custom-call(bf16[32,16,768]{2,1,0:T(8,128)(2,1)S(1)} %all-to-all-done.1.x_ref, bf16[512,512]{1,0:T(8,128)(2,1)S(1)} %copy-done, bf16[12,65536]{1,0:T(8,128)(2,1)} %weave.2.refs_0_), custom_call_target="tpu_custom_call", output_to_operand_aliasing={{}: (2, {})} | custom-call | tf_op jit(solution)/shard_map/weave/pallas_call | solution.py:234
  (49 shorter events, 0.8 us)
Async XLA Ops:
  2.0 25.3 %copy-start.1 = (bf16[2048,384]{1,0:T(8,128)(2,1)S(1)}, bf16[2048,384]{1,0:T(8,128)(2,1)}, u32[]{:S(2)}) copy-start(bf16[2048,384]{1,0:T(8,128)(2,1)} %param.11) | copy-start | bytes 4718596
  2.1 12.6 %collective-permute-start.1 = (bf16[112,384]{1,0:T(8,128)(2,1)S(1)}, bf16[112,384]{1,0:T(8,128)(2,1)S(1)}, u32[]{:S(2)}, u32[]{:S(2)}) collective-permute-start(bf16[112,384]{1,0:T(8,128)(2,1)S(1)} %constant_dynamic-slice_fusion.15), channel_id=1, source_target_pairs={{0,8},{1,9},{2,10},{3,11},{4,12},{5,13},{6,14},{7,15},{8,0},{9,1},... | collective-permute-start | bytes 258056 | tf_op jit(solution)/shard_map/ppermute | solution.py:270
  5.2 4.3 %collective-permute-start = (bf16[16,384]{1,0:T(8,128)(2,1)S(1)}, bf16[16,384]{1,0:T(8,128)(2,1)S(1)}, u32[]{:S(2)}, u32[]{:S(2)}) collective-permute-start(bf16[16,384]{1,0:T(8,128)(2,1)S(1)} %get-tuple-element.14), channel_id=1, source_target_pairs={{0,8},{1,9},{2,10},{3,11},{4,12},{5,13},{6,14},{7,15},{8,0},{9,1},... | collective-permute-start | bytes 36872 | tf_op jit(solution)/shard_map/ppermute | solution.py:269
  5.3 9.4 %collective-permute-start.3 = (bf16[128,384]{1,0:T(8,128)(2,1)S(1)}, bf16[128,384]{1,0:T(8,128)(2,1)S(1)}, u32[]{:S(2)}, u32[]{:S(2)}) collective-permute-start(bf16[128,384]{1,0:T(8,128)(2,1)S(1)} %get-tuple-element.19), channel_id=1, source_target_pairs={{0,24},{1,25},{2,26},{3,27},{4,28},{5,29},{6,30},{7,31},{8,16},{9,... | collective-permute-start | bytes 294920 | tf_op jit(solution)/shard_map/ppermute | solution.py:272
  9.4 8.0 %collective-permute-start.2 = (bf16[128,384]{1,0:T(8,128)(2,1)S(1)}, bf16[128,384]{1,0:T(8,128)(2,1)S(1)}, u32[]{:S(2)}, u32[]{:S(2)}) collective-permute-start(bf16[128,384]{1,0:T(8,128)(2,1)S(1)} %get-tuple-element.20), channel_id=1, source_target_pairs={{0,16},{1,17},{2,18},{3,19},{4,20},{5,21},{6,22},{7,23},{8,24},{9,... | collective-permute-start | bytes 294920 | tf_op jit(solution)/shard_map/ppermute | solution.py:272
  9.4 19.3 %all-to-all-start.2 = ((bf16[32,16,384]{2,1,0:T(8,128)(2,1)}), bf16[32,16,384]{2,1,0:T(8,128)(2,1)S(1)}, u32[]{:S(2)}, u32[]{:S(2)}) async-start(bf16[32,16,384]{2,1,0:T(8,128)(2,1)} %get-tuple-element.10), calls=%async_computation.2 | async-start | bytes 786432 | tf_op jit(solution)/shard_map/all_to_all | solution.py:250
  17.4 6.8 %collective-permute-start.4 = (bf16[128,384]{1,0:T(8,128)(2,1)S(1)}, bf16[128,384]{1,0:T(8,128)(2,1)S(1)}, u32[]{:S(2)}, u32[]{:S(2)}) collective-permute-start(bf16[128,384]{1,0:T(8,128)(2,1)S(1)} %pad_maximum_fusion), channel_id=1, source_target_pairs={{0,2},{1,3},{2,0},{3,1},{4,6},{5,7},{6,4},{7,5},{8,10},{9,11},{10,... | collective-permute-start | bytes 294920 | tf_op jit(solution)/shard_map/ppermute | solution.py:272
  19.0 6.3 %collective-permute-start.5 = (bf16[128,384]{1,0:T(8,128)(2,1)S(1)}, bf16[128,384]{1,0:T(8,128)(2,1)S(1)}, u32[]{:S(2)}, u32[]{:S(2)}) collective-permute-start(bf16[128,384]{1,0:T(8,128)(2,1)S(1)} %pad_maximum_fusion.1), channel_id=1, source_target_pairs={{0,4},{1,5},{2,6},{3,7},{4,0},{5,1},{6,2},{7,3},{8,12},{9,13},{10,... | collective-permute-start | bytes 294920 | tf_op jit(solution)/shard_map/ppermute | solution.py:272
  20.6 6.5 %collective-permute-start.6 = (bf16[128,384]{1,0:T(8,128)(2,1)S(1)}, bf16[128,384]{1,0:T(8,128)(2,1)S(1)}, u32[]{:S(2)}, u32[]{:S(2)}) collective-permute-start(bf16[128,384]{1,0:T(8,128)(2,1)S(1)} %pad_maximum_fusion.2), channel_id=1, source_target_pairs={{0,6},{1,7},{2,4},{3,5},{4,2},{5,3},{6,0},{7,1},{8,14},{9,15},{10,... | collective-permute-start | bytes 294920 | tf_op jit(solution)/shard_map/ppermute | solution.py:272
  27.2 5.0 %copy-start.4 = (bf16[256,384]{1,0:T(8,128)(2,1)}, bf16[256,384]{1,0:T(8,128)(2,1)S(1)}, u32[]{:S(2)}) copy-start(bf16[256,384]{1,0:T(8,128)(2,1)S(1)} %get-tuple-element.48.refs_1_) | copy-start | bytes 589828
  27.2 1.5 %collective-permute-start.7 = (bf16[256,384]{1,0:T(8,128)(2,1)S(1)}, bf16[256,384]{1,0:T(8,128)(2,1)S(1)}, u32[]{:S(2)}, u32[]{:S(2)}) collective-permute-start(bf16[256,384]{1,0:T(8,128)(2,1)S(1)} %get-tuple-element.49), channel_id=1, source_target_pairs={{0,1},{1,0},{2,3},{3,2},{4,5},{5,4},{6,7},{7,6},{8,9},{9,8},{10,11... | collective-permute-start | bytes 589832 | tf_op jit(solution)/shard_map/ppermute | solution.py:272
  28.7 3.5 %copy-start.5 = (bf16[256,384]{1,0:T(8,128)(2,1)}, bf16[256,384]{1,0:T(8,128)(2,1)S(1)}, u32[]{:S(2)}) copy-start(bf16[256,384]{1,0:T(8,128)(2,1)S(1)} %collective-permute-done.7.refs_2_) | copy-start | bytes 589828
  28.7 3.5 %copy-start.3 = (bf16[32,16,384]{2,1,0:T(8,128)(2,1)}, bf16[32,16,384]{2,1,0:T(8,128)(2,1)S(1)}, u32[]{:S(2)}) copy-start(bf16[32,16,384]{2,1,0:T(8,128)(2,1)S(1)} %all-to-all-done.2) | copy-start | bytes 1179652
  28.7 24.1 %all-to-all-start = ((bf16[32,32,384]{2,1,0:T(8,128)(2,1)}), bf16[32,32,384]{2,1,0:T(8,128)(2,1)S(1)}, u32[]{:S(2)}, u32[]{:S(2)}) async-start(bf16[32,32,384]{2,1,0:T(8,128)(2,1)} %bitcast.5), calls=%async_computation | async-start | bytes 1572864 | tf_op jit(solution)/shard_map/all_to_all | solution.py:250
  52.8 3.6 %copy-start.2 = (bf16[32,32,384]{2,1,0:T(8,128)(2,1)}, bf16[32,32,384]{2,1,0:T(8,128)(2,1)S(1)}, u32[]{:S(2)}) copy-start(bf16[32,32,384]{2,1,0:T(8,128)(2,1)S(1)} %all-to-all-done) | copy-start | bytes 2359300
  52.8 24.2 %all-to-all-start.3 = ((bf16[32,16,768]{2,1,0:T(8,128)(2,1)}), bf16[32,16,768]{2,1,0:T(8,128)(2,1)S(1)}, u32[]{:S(2)}, u32[]{:S(2)}) async-start(bf16[32,16,768]{2,1,0:T(8,128)(2,1)} %bitcast.21), calls=%async_computation.3 | async-start | bytes 1572864 | tf_op jit(solution)/shard_map/all_to_all | solution.py:250
  56.5 24.2 %copy-start = (bf16[512,512]{1,0:T(8,128)(2,1)S(1)}, bf16[512,512]{1,0:T(8,128)(2,1)}, u32[]{:S(2)}) copy-start(bf16[512,512]{1,0:T(8,128)(2,1)} %constant.135.clone.weave_ref) | copy-start | bytes 1572868
  77.1 24.2 %all-to-all-start.1 = ((bf16[32,16,768]{2,1,0:T(8,128)(2,1)}), bf16[32,16,768]{2,1,0:T(8,128)(2,1)S(1)}, u32[]{:S(2)}, u32[]{:S(2)}) async-start(bf16[32,16,768]{2,1,0:T(8,128)(2,1)} %bitcast.22), calls=%async_computation.1 | async-start | bytes 1572864 | tf_op jit(solution)/shard_map/all_to_all | solution.py:250
